TPU v7x, 32 devices: a whole 2x2x4 slice. The times are simulated.
32 devices in a mesh: pipe: 8 (over z, core), seq: 4 (over y, x).
Axes of the slice: x: 2, y: 2, z: 4, core: 2. Of those that a mesh axis runs over, the one named last changes fastest.
Arguments:
- x_fwd: float32 [8, 512, 2048], P('pipe', 'seq'), may hold values from -12 to 12
- x_bwd: float32 [8, 512, 2048], P('pipe', 'seq'), may hold values from -12 to 12
- grad_in: float32 [8, 512, 2048], P('pipe', 'seq'), may hold values from -6 to 6
- gain: float32 [8, 2048], P('pipe'), may hold values from 0.25 to 1.75
- w_query: bfloat16 [8, 2048, 2048], P('pipe', None, 'seq'), may hold values from -2 to 2
- w_key: bfloat16 [8, 2048, 2048], P('pipe', None, 'seq'), may hold values from -2 to 2
- w_value: bfloat16 [8, 2048, 2048], P('pipe', None, 'seq'), may hold values from -0.125 to 0.125
- w_out: bfloat16 [8, 2048, 2048], P('pipe', None, 'seq'), may hold values from -0.125 to 0.125
Outputs:
- act_next: float32 [8, 512, 2048], P('pipe', 'seq')
- grad_prev: float32 [8, 512, 2048], P('pipe', 'seq')
All inputs are finite; a program needn't handle non-finite values.
Results may differ from a plain program's by a relative error of at most 0.012.
The roundings to bfloat16 on the way count: a program that leaves them out, or rounds other values in their place, can miss the bound.
Values may be sent and summed in bfloat16 or wider, within the bound.
No kernel may reach another device: no remote copies, remote signals or barrier semaphores. Data moves between devices by JAX's collectives and lax.ppermute only.
A program may use at most 192 MiB of HBM per device.

v0:
```python
import functools
import math

import jax
import jax.numpy as jnp
from jax import lax
from jax.experimental import pallas as pl
from jax.experimental.pallas import tpu as pltpu
from jax.sharding import PartitionSpec as P

HD = 128
LANES = 128
CHUNK = 256
EXP2_SCALE = HD ** (-0.5) * math.log2(math.e)
NT = (((1,), (1,)), ((), ()))
TN = (((0,), (0,)), ((), ()))
HEADS_WEIGHT = 8_000_000_000
TERMS_WEIGHT = 3_000_000_000
INPUT_GRAD_WEIGHT = 8_000_000_000
LAST_SUM_WEIGHT = 8_000_000_000
FORWARD_WEIGHT = 5_000_000_000
SUMS_WEIGHT = 6000000000
MIB = 1024 * 1024


def bits_of(number):
    return [bit for bit in range(number.bit_length()) if (number >> bit) & 1]


def by_distance(count):
    return sorted(range(1, count), key=lambda rel: (len(bits_of(rel)), rel))


def part_bounds(rows, count):
    parts = 2 if count > 2 else 1
    return [(rows * i // parts, rows * (i + 1) // parts) for i in range(parts)]


def last_bit(rel, part):
    bits = bits_of(rel)
    return bits[part % len(bits)]


def ways_to(rel, bounds):
    ways = {}
    for part, (low, high) in enumerate(bounds):
        bit = last_bit(rel, part)
        ways[bit] = (min(low, ways.get(bit, (low, high))[0]), high)
    return [(bit, low, high) for bit, (low, high) in ways.items()]


def across(value, bit):
    count = lax.axis_size("seq")
    return lax.ppermute(value, "seq", [(i, i ^ (1 << bit)) for i in range(count)])


def across_and_on(value, flip):
    count, sections = lax.axis_size("seq"), lax.axis_size("pipe")
    pairs = [
        (p * count + i, (p + 1) % sections * count + (i ^ flip))
        for p in range(sections)
        for i in range(count)
    ]
    return lax.ppermute(value, ("pipe", "seq"), pairs)


def passed_along(value, axis, steps):
    count = lax.axis_size(axis)
    pairs = [(source, (source + steps) % count) for source in range(count)]
    return lax.ppermute(value, axis, pairs)


def onward_rows(count, bounds):
    return [
        (rel ^ (1 << bit), bit, low, high)
        for rel in by_distance(count)
        for bit, low, high in ways_to(rel, bounds)
    ]


def goes_on(rel, low, count, bounds):
    return any(
        rel == at and first <= low < last for at, _, first, last in onward_rows(count, bounds)
    )


def gather_first(own, what):
    count = lax.axis_size("seq")
    blocks = {(0, 0): own}
    for rel in by_distance(count):
        if len(bits_of(rel)) == 1:
            with jax.named_scope(f"gather_{what}_block{rel}"):
                blocks[rel, 0] = across(own, bits_of(rel)[0])
    return blocks


def gather_parts(blocks, own_parts, bounds, early, what):
    count = lax.axis_size("seq")
    for rel in by_distance(count):
        for value, (low, _) in zip(own_parts, bounds):
            blocks.setdefault((0, low), value)
            if len(bits_of(rel)) == 1 and goes_on(rel, low, count, bounds) == early:
                with jax.named_scope(f"gather_{what}_block{rel}_first{low}"):
                    blocks[rel, low] = across(value, bits_of(rel)[0])
    return blocks


def second_hops(blocks, bounds):
    hops = []
    for rel, _, low, high in onward_rows(lax.axis_size("seq"), bounds):
        if len(bits_of(rel)) == 1:
            first = low if (rel, low) in blocks else 0
            hops.append((blocks[rel, first], low - first, high - first))
    return hops


def gather_rest(blocks, picked, bounds, what):
    count = lax.axis_size("seq")
    picked = list(picked)
    for rel, bit, low, high in onward_rows(count, bounds):
        if rel == 0:
            continue
        value = picked.pop(0) if len(bits_of(rel)) == 1 else blocks[rel, low]
        if value.shape[0] > high - low:
            value = value[: high - low]
        with jax.named_scope(f"gather_{what}_block{rel ^ (1 << bit)}_row{low}"):
            blocks[rel ^ (1 << bit), low] = across(value, bit)
    return blocks


def messages_of(rows, count, joined):
    parts = range(len(part_bounds(rows, count)))
    later = {
        (rel ^ (1 << last_bit(rel, part)), part)
        for rel in range(1, count)
        for part in parts
        if len(bits_of(rel)) > 1
    }
    groups, waiting = {}, {}
    for rel in reversed(by_distance(count)):
        for part in parts:
            key = (rel, part)
            if not joined and len(bits_of(rel)) == 1:
                waiting.setdefault(rel, []).append(key)
            elif key in later:
                waiting[key] = [key]
            else:
                groups.setdefault(last_bit(*key) if joined else key, []).append(key)
    return list(groups.values()), list(waiting.values())


class Scatter:

    def __init__(self, terms, rows, joined, send_last, what):
        count = lax.axis_size("seq")
        self.bounds = part_bounds(rows, count)
        self.groups, waiting = messages_of(rows, count, joined)
        self.leaving = list(terms[: len(self.groups)])
        self.waiting = list(zip(waiting, terms[len(self.groups) :]))
        self.send_last, self.what = send_last, what
        self.arrived, self.final = {}, {}

    def send(self, value, keys):
        bit = last_bit(*keys[0])
        targets = [(rel ^ (1 << bit), part) for rel, part in keys]
        onward = any(rel for rel, _ in targets)
        with jax.named_scope(f"scatter_{self.what}_block{keys[0][0]}_part{keys[0][1]}"):
            moved = (across if onward else self.send_last)(value, bit)
        first = 0
        for key, target in zip(keys, targets):
            if target[0]:
                self.arrived.setdefault(target, []).append((moved, first))
            else:
                self.final[key] = (moved, first)
            first += self.bounds[key[1]][1] - self.bounds[key[1]][0]

    def send_groups(self):
        for value, keys in zip(self.leaving, self.groups):
            self.send(value, keys)

    def send_sums(self, after=(), weight=1):
        sums = []
        height = self.bounds[0][1] - self.bounds[0][0]
        levels = {len(bits_of(keys[0][0])) for keys, _ in self.waiting}
        for level in sorted(levels, reverse=True):
            found = [pair for pair in self.waiting if len(bits_of(pair[0][0][0])) == level]
            totals = [
                (term, [self.arrived.get(key, []) for key in keys]) for keys, term in found
            ]
            results = sum_rows(totals, height, after, weight)
            sums += results
            for (keys, _), value in zip(found, results):
                self.send(value, keys)
        return sums


def call(kernel, out_shapes, operands, in_specs, scratch=(), flops=1, vmem=10, name=None):
    return pl.pallas_call(
        kernel,
        out_shape=out_shapes,
        in_specs=in_specs,
        out_specs=[pl.BlockSpec(memory_space=pltpu.VMEM)] * len(out_shapes),
        scratch_shapes=list(scratch),
        compiler_params=pltpu.CompilerParams(vmem_limit_bytes=vmem * MIB),
        cost_estimate=pl.CostEstimate(flops=int(flops), bytes_accessed=1, transcendentals=0),
        name=name,
    )(*operands)


ANY = pl.BlockSpec(memory_space=pl.ANY)
HBM = pl.BlockSpec(memory_space=pltpu.HBM)
VMEM = pl.BlockSpec(memory_space=pltpu.VMEM)


def normed_rows(inputs, gain, bounds, after=(), vmem=10):
    rows, width = inputs.shape

    def kernel(x_any, gain_any, *refs):
        *outs, inv_ref, x_ref, gain_ref, sems = refs[len(after) :]
        copies = [
            pltpu.make_async_copy(source, held, sems.at[i])
            for i, (source, held) in enumerate([(x_any, x_ref), (gain_any, gain_ref)])
        ]
        for copy in copies:
            copy.start()
        for copy in copies:
            copy.wait()
        for out_ref, (low, high) in zip(outs, bounds):
            x = x_ref[low:high, :]
            inv = lax.rsqrt(jnp.mean(x * x, -1, keepdims=True) + 1e-05)
            out_ref[...] = (x * inv * gain_ref[...]).astype(jnp.bfloat16)
            inv_ref[low:high, :] = inv

    *parts, inv = call(
        kernel,
        [jax.ShapeDtypeStruct((high - low, width), jnp.bfloat16) for low, high in bounds]
        + [jax.ShapeDtypeStruct((rows, 1), jnp.float32)],
        [inputs, gain, *after],
        [HBM] * 2 + [ANY] * len(after),
        [
            pltpu.VMEM(inputs.shape, jnp.float32),
            pltpu.VMEM(gain.shape, jnp.float32),
            pltpu.SemaphoreType.DMA((2,)),
        ],
        vmem=vmem,
        name="norm",
    )
    return parts, inv


def picked_rows(pieces, after=()):
    n = len(pieces)

    def kernel(*refs):
        outs, sems = refs[n + len(after) : -1], refs[-1]
        copies = [
            pltpu.make_async_copy(ref.at[pl.ds(low, high - low), :], out_ref, sems.at[i])
            for i, (ref, out_ref, (_, low, high)) in enumerate(zip(refs, outs, pieces))
        ]
        for copy in copies:
            copy.start()
        for copy in copies:
            copy.wait()

    return call(
        kernel,
        [
            jax.ShapeDtypeStruct((high - low, value.shape[1]), value.dtype)
            for value, low, high in pieces
        ],
        [value for value, _, _ in pieces] + list(after),
        [ANY] * (n + len(after)),
        [pltpu.SemaphoreType.DMA((n,))],
        name="pick",
    )


def cast_rows(inputs, after=()):
    def kernel(x_ref, *refs):
        refs[len(after)][...] = x_ref[...].astype(jnp.bfloat16)

    return call(
        kernel,
        [jax.ShapeDtypeStruct(inputs.shape, jnp.bfloat16)],
        (inputs, *after),
        [VMEM] + [ANY] * len(after),
        name="cast",
    )[0]


def sum_rows(totals, height, after=(), weight=1):
    pieces = [piece for _, parts in totals for moved in parts for piece in moved]
    n, m = len(totals), len(pieces)

    def kernel(*refs):
        arrivals, outs = list(refs[n : n + m]), refs[-n:]
        for (_, parts), term_ref, out_ref in zip(totals, refs, outs):
            for i, moved in enumerate(parts):
                here = slice(i * height, (i + 1) * height)
                total = term_ref[here, :]
                for _, first in moved:
                    ref = arrivals.pop(0)
                    total = total + ref[first : first + height, :].astype(jnp.float32)
                out_ref[here, :] = total.astype(jnp.bfloat16)

    return call(
        kernel,
        [jax.ShapeDtypeStruct(term.shape, jnp.bfloat16) for term, _ in totals],
        [term for term, _ in totals] + [value for value, _ in pieces] + list(after),
        [VMEM] * (n + m) + [ANY] * len(after),
        flops=weight,
        name="sum_rows",
    )


def block_copies(block_refs, keys, rows, all_rows, sems):
    return [
        pltpu.make_async_copy(
            ref, all_rows.at[pl.ds(rel * rows + low, ref.shape[0]), :], sems.at[i]
        )
        for i, (ref, (rel, low)) in enumerate(zip(block_refs, keys))
    ]


def turned(values, cosine, sine):
    return values * cosine + pltpu.roll(values, HD // 2, 1) * sine


def project_into(rows_ref, weight_ref, out_ref, cos_ref=None, sin_ref=None):
    features = out_ref.shape[1]
    for low in range(0, features, CHUNK):
        high = min(low + CHUNK, features)
        values = jnp.dot(
            rows_ref[...], weight_ref[:, low:high], preferred_element_type=jnp.float32
        )
        for head in range(0, high - low, HD):
            piece = values[:, head : head + HD]
            if cos_ref is not None:
                piece = turned(piece, cos_ref[...], sin_ref[...])
            out_ref[:, low + head : low + head + HD] = piece.astype(jnp.bfloat16)


def project(blocks, weights, cosine, sine, rows, weight=1):
    keys = sorted(blocks)
    length, width = cosine.shape[0], blocks[0, 0].shape[1]
    features = weights[0].shape[1]
    n = len(keys)

    def kernel(*refs):
        block_refs, weight_refs = refs[:n], refs[n : n + 3]
        cos_ref, sin_ref = refs[n + 3 : n + 5]
        outs = refs[n + 5 : n + 8]
        all_rows, sems = refs[n + 8 :]
        copies = block_copies(block_refs, keys, rows, all_rows, sems)
        for copy in copies:
            copy.start()
        for copy in copies:
            copy.wait()
        for i in range(3):
            tables = (cos_ref, sin_ref) if i < 2 else ()
            project_into(all_rows, weight_refs[i], outs[i], *tables)

    return call(
        kernel,
        [jax.ShapeDtypeStruct((length, features), jnp.bfloat16)] * 3,
        [blocks[key] for key in keys] + list(weights) + [cosine, sine],
        [ANY] * n + [VMEM] * 5,
        [pltpu.VMEM((length, width), jnp.bfloat16), pltpu.SemaphoreType.DMA((n,))],
        flops=weight,
        vmem=20,
        name="project",
    )


def term_outs(rows, width, count, joined):
    bounds = part_bounds(rows, count)
    groups, waiting = messages_of(rows, count, joined)

    def shape(keys, dtype):
        height = sum(bounds[part][1] - bounds[part][0] for _, part in keys)
        return jax.ShapeDtypeStruct((height, width), dtype)

    return [shape(keys, jnp.bfloat16) for keys in groups] + [
        shape(keys, jnp.float32) for keys in waiting
    ]


def store_terms(values, low, refs, rows, count, joined):
    bounds = part_bounds(rows, count)
    groups, waiting = messages_of(rows, count, joined)
    for ref, keys in zip(refs, groups + waiting):
        at = 0
        for rel, part in keys:
            first, last = bounds[part]
            piece = values[rel * rows + first : rel * rows + last]
            ref[at : at + last - first, low : low + values.shape[1]] = piece.astype(ref.dtype)
            at += last - first


def backward_heads(blocks, qkv, weight, cosine, sine, rows):
    in_keys = sorted(blocks)
    length, width = cosine.shape[0], blocks[0, 0].shape[1]
    features = qkv[0].shape[1]
    n = len(in_keys)
    step = min(length, 512)

    def kernel(*refs):
        block_refs, weight_ref = refs[:n], refs[n]
        q_ref, k_ref, v_ref, cos_ref, sin_ref = refs[n + 1 : n + 6]
        d_qkv = refs[n + 6 : n + 9]
        all_rows, d_attn, sems = refs[n + 9 :]
        copies = block_copies(block_refs, in_keys, rows, all_rows, sems)
        for copy in copies:
            copy.start()
        for copy in copies:
            copy.wait()
        project_into(all_rows, weight_ref, d_attn)

        for head in range(features // HD):
            cols = slice(head * HD, (head + 1) * HD)
            key, value = k_ref[:, cols], v_ref[:, cols]
            d_key, d_value = 0.0, 0.0
            for low in range(0, length, step):
                part = slice(low, low + step)
                query, grad = q_ref[part, cols], d_attn[part, cols]
                scores = lax.dot_general(key, query, NT, preferred_element_type=jnp.float32)
                top = jnp.max(scores, 0, keepdims=True)
                raised = jnp.exp2((scores - top) * EXP2_SCALE)
                probs = raised * (1.0 / jnp.sum(raised, 0, keepdims=True))
                d_value += jnp.dot(
                    probs.astype(jnp.bfloat16), grad, preferred_element_type=jnp.float32
                )
                d_probs = lax.dot_general(value, grad, NT, preferred_element_type=jnp.float32)
                delta = jnp.sum(probs * d_probs, 0, keepdims=True)
                d_scores = (probs * (d_probs - delta) * HD ** (-0.5)).astype(jnp.bfloat16)
                d_key += jnp.dot(d_scores, query, preferred_element_type=jnp.float32)
                d_query = lax.dot_general(
                    key, d_scores, TN, preferred_element_type=jnp.float32
                ).T
                d_qkv[0][part, cols] = turned(
                    d_query, cos_ref[part, :], -sin_ref[part, :]
                ).astype(jnp.bfloat16)
            d_qkv[1][:, cols] = turned(d_key, cos_ref[...], -sin_ref[...]).astype(jnp.bfloat16)
            d_qkv[2][:, cols] = d_value.astype(jnp.bfloat16)

    return call(
        kernel,
        [jax.ShapeDtypeStruct((length, features), jnp.bfloat16)] * 3,
        [blocks[key] for key in in_keys] + [weight] + list(qkv) + [cosine, sine],
        [ANY] * n + [VMEM] * 6,
        [
            pltpu.VMEM((length, width), jnp.bfloat16),
            pltpu.VMEM((length, features), jnp.bfloat16),
            pltpu.SemaphoreType.DMA((n,)),
        ],
        vmem=28,
        flops=HEADS_WEIGHT,
        name="backward_heads",
    )


def backward_terms(d_qkv, weights, rows, count, joined, after=()):
    length, features = d_qkv[0].shape
    width = weights[0].shape[0]
    shapes = term_outs(rows, width, count, joined)

    def kernel(*refs):
        grads, weight_refs = refs[:3], refs[3:6]
        own_ref, *outs = refs[6 + len(after) :]
        for low in range(0, width, CHUNK):
            total = 0.0
            for i in range(3):
                total += lax.dot_general(
                    grads[i][...],
                    weight_refs[i][low : low + CHUNK, :],
                    NT,
                    preferred_element_type=jnp.float32,
                )
            own_ref[:, low : low + CHUNK] = total[:rows]
            store_terms(total, low, outs, rows, count, joined)

    own, *terms = call(
        kernel,
        [jax.ShapeDtypeStruct((rows, width), jnp.float32)] + shapes,
        list(d_qkv) + list(weights) + list(after),
        [VMEM] * 6 + [ANY] * len(after),
        vmem=24,
        flops=TERMS_WEIGHT,
        name="backward_terms",
    )
    return own, terms


def forward_terms(qkv, act_in, weight, rows, count, joined, after=()):
    length, features = qkv[0].shape
    width = weight.shape[0]
    shapes = term_outs(rows, width, count, joined)
    step = min(length, 512)

    def kernel(*refs):
        q_ref, k_ref, v_ref, act_ref, weight_ref = refs[:5]
        own_ref, *outs = refs[5 + len(after) : -1]
        attn = refs[-1]
        for head in range(features // HD):
            cols = slice(head * HD, (head + 1) * HD)
            for low in range(0, length, step):
                part = slice(low, low + step)
                scores = lax.dot_general(
                    q_ref[part, cols], k_ref[:, cols], NT, preferred_element_type=jnp.float32
                )
                top = jnp.max(scores, 1, keepdims=True)
                raised = jnp.exp2((scores - top) * EXP2_SCALE)
                total = jnp.sum(raised, 1, keepdims=True)
                mixed = jnp.dot(
                    raised.astype(jnp.bfloat16), v_ref[:, cols], preferred_element_type=jnp.float32
                )
                attn[part, cols] = (mixed * (1.0 / total)).astype(jnp.bfloat16)

        for low in range(0, width, CHUNK):
            total = lax.dot_general(
                attn[...], weight_ref[low : low + CHUNK, :], NT, preferred_element_type=jnp.float32
            )
            own = total[:rows] + act_ref[:, low : low + CHUNK]
            own_ref[:, low : low + CHUNK] = own.astype(jnp.bfloat16)
            store_terms(total, low, outs, rows, count, joined)

    own, *terms = call(
        kernel,
        [jax.ShapeDtypeStruct((rows, width), jnp.bfloat16)] + shapes,
        list(qkv) + [act_in, weight, *after],
        [VMEM] * 5 + [ANY] * len(after),
        [pltpu.VMEM((length, features), jnp.bfloat16)],
        vmem=24,
        flops=FORWARD_WEIGHT,
        name="forward_terms",
    )
    return own, terms


def input_grad(own, pieces, saved, grad, inv, gain, bounds, after=()):
    keys = sorted(pieces)

    def kernel(own_ref, saved_ref, grad_ref, inv_ref, gain_ref, *refs):
        out_ref = refs[-1]
        for part, (low, high) in enumerate(bounds):
            total = own_ref[low:high, :]
            for ref, key in zip(refs, keys):
                if key[1] == part:
                    first = pieces[key][1]
                    total = total + ref[first : first + high - low, :].astype(jnp.float32)
            total = total * gain_ref[...]
            saved_rows = saved_ref[low:high, :]
            mean = jnp.mean(saved_rows * total, -1, keepdims=True)
            inv_rows = inv_ref[low:high, :]
            out_ref[low:high, :] = (
                grad_ref[low:high, :]
                + inv_rows * total
                - saved_rows * (inv_rows * inv_rows * inv_rows * mean)
            ).astype(jnp.bfloat16)

    return call(
        kernel,
        [jax.ShapeDtypeStruct(own.shape, jnp.bfloat16)],
        [own, saved, grad, inv, gain] + [pieces[key][0] for key in keys] + list(after),
        [VMEM] * (5 + len(keys)) + [ANY] * len(after),
        flops=INPUT_GRAD_WEIGHT,
        name="input_grad",
    )[0]


def added_pieces(total, pieces, refs, part, height):
    for ref, (key, (_, first)) in zip(refs, pieces.items()):
        if key[1] == part:
            total = total + ref[first : first + height, :].astype(jnp.float32)
    return total


def activation_sum(base, pieces, bounds):
    def kernel(base_ref, *refs):
        out_ref, mark_ref = refs[-2:]
        for part, (low, high) in enumerate(bounds):
            total = base_ref[low:high, :].astype(jnp.float32)
            out_ref[0, low:high, :] = added_pieces(total, pieces, refs, part, high - low)
        mark_ref[...] = jnp.zeros_like(mark_ref)

    return call(
        kernel,
        [
            jax.ShapeDtypeStruct((1, *base.shape), jnp.float32),
            jax.ShapeDtypeStruct((8, LANES), jnp.float32),
        ],
        [base] + [value for value, _ in pieces.values()],
        [VMEM] * (1 + len(pieces)),
        flops=LAST_SUM_WEIGHT,
        name="activation_sum",
    )


def widened(values, bounds, after=()):
    def kernel(in_any, *refs):
        out_ref, held, sems = refs[-3:]
        copies = [
            pltpu.make_async_copy(
                in_any.at[pl.ds(low, high - low), :],
                held.at[pl.ds(low, high - low), :],
                sems.at[i],
            )
            for i, (low, high) in enumerate(bounds)
        ]
        for copy in copies:
            copy.start()
        for copy, (low, high) in zip(copies, bounds):
            copy.wait()
            out_ref[0, low:high, :] = held[low:high, :].astype(jnp.float32)

    return call(
        kernel,
        [jax.ShapeDtypeStruct((1, *values.shape), jnp.float32)],
        [values, *after],
        [ANY] * (1 + len(after)),
        [
            pltpu.VMEM(values.shape, values.dtype),
            pltpu.SemaphoreType.DMA((len(bounds),)),
        ],
        name="widen",
    )[0]


def rope_tables(positions):
    half_dim = HD // 2
    inverse = 10000.0 ** (-(jnp.arange(half_dim).astype(jnp.float32) * 2.0 / HD))
    angles = positions.astype(jnp.float32)[:, None] * inverse[None, :]
    cosine, sine = jnp.cos(angles), jnp.sin(angles)
    return jnp.concatenate([cosine, cosine], 1), jnp.concatenate([-sine, sine], 1)


def shards(x_fwd, x_bwd, grad_in, gain, w_query, w_key, w_value, w_out):
    act_in, saved_in, grad = x_fwd[0], x_bwd[0], grad_in[0]
    rows = act_in.shape[0]
    count = lax.axis_size("seq")
    bounds = part_bounds(rows, count)
    own_query, own_key, own_value, own_out = w_query[0], w_key[0], w_value[0], w_out[0]

    block_of = lax.axis_index("seq") ^ jnp.arange(count)
    positions = (block_of[:, None] * rows + jnp.arange(rows)[None, :]).reshape(-1)
    cosine, sine = rope_tables(positions)

    whole = [(0, rows)]
    projections = (own_query, own_key, own_value)
    (normed_bwd,), inv_bwd = normed_rows(saved_in, gain, whole, vmem=62)
    grad_low = cast_rows(grad, [normed_bwd])
    all_bwd = gather_first(normed_bwd, "saved")
    all_grad = gather_first(grad_low, "grad")
    normed_fwd, _ = normed_rows(act_in, gain, bounds)
    picked = picked_rows(second_hops(all_bwd, bounds), [grad_low])
    all_bwd = gather_rest(all_bwd, picked, bounds, "saved")
    n = len(bounds)
    handed_on = [(value, 0, value.shape[0]) for value in normed_fwd]
    picked = picked_rows(handed_on + second_hops(all_grad, bounds), picked)
    all_fwd = gather_parts({}, picked[:n], bounds, True, "input")
    all_grad = gather_rest(all_grad, picked[n:], bounds, "grad")

    qkv = project(all_bwd, projections, cosine, sine, rows)
    all_fwd = gather_parts(all_fwd, picked_rows(handed_on, qkv[:1]), bounds, False, "input")
    d_qkv = backward_heads(all_grad, qkv, own_out, cosine, sine, rows)
    picked = picked_rows(second_hops(all_fwd, bounds), d_qkv[:1])
    all_fwd = gather_rest(all_fwd, picked, bounds, "input")
    d_own, d_terms = backward_terms(d_qkv, projections, rows, count, True, picked)
    qkv = project(all_fwd, projections, cosine, sine, rows, FORWARD_WEIGHT)
    own, terms = forward_terms(qkv, act_in, own_out, rows, count, False)

    back = Scatter(d_terms, rows, True, across, "grad")
    front = Scatter(
        terms, rows, False, lambda value, bit: across_and_on(value, 1 << bit), "branch"
    )
    back.send_groups()
    front.send_groups()
    d_sums = back.send_sums([terms[0]])
    own = across_and_on(own, 0)
    sums = front.send_sums(d_sums, SUMS_WEIGHT)
    d_input = input_grad(
        d_own, back.final, saved_in, grad, inv_bwd, gain, bounds, [own, *sums]
    )
    act_next, mark = activation_sum(own, front.final, bounds)
    return (act_next, widened(passed_along(d_input, "pipe", -1), bounds, [mark]))


def solution(mesh):
    placed = (
        P("pipe", "seq", None),
        P("pipe", "seq", None),
        P("pipe", "seq", None),
        P("pipe", None),
        P("pipe", None, "seq"),
        P("pipe", None, "seq"),
        P("pipe", None, "seq"),
        P("pipe", None, "seq"),
    )
    return jax.shard_map(
        shards,
        mesh=mesh,
        in_specs=placed,
        out_specs=(P("pipe", "seq", None), P("pipe", "seq", None)),
        check_vma=False,
    )
```

profile of v0, /device:TPU:0, one launch (start us, length us, event | category | flops | bytes accessed | tf_op | source)
XLA Modules:
  0.0 102.8 jit_solution(14900412622583816638)
XLA Ops:
  0.6 2.3 %norm.3 = (bf16[128,2048]{1,0:T(8,128)(2,1)}, f32[128,1]{1,0:T(8,128)}) custom-call(f32[128,2048]{1,0:T(8,128)} %bitcast.22, f32[1,2048]{1,0:T(1,128)} %gain_ref.1), custom_call_target="tpu_custom_call" | custom-call | flops 1 | bytes 1 | tf_op jit(solution)/shard_map/norm/pallas_call | solution.py:198
  2.9 3.0 %collective-permute-start.3 = (bf16[128,2048]{1,0:T(8,128)(2,1)}, bf16[128,2048]{1,0:T(8,128)(2,1)S(1)}, u32[]{:S(2)}, u32[]{:S(2)}) collective-permute-start(bf16[128,2048]{1,0:T(8,128)(2,1)} %get-tuple-element.43.refs_0_), channel_id=1, source_target_pairs={{0,1},{1,0},{2,3},{3,2},{4,5},{5,4},{6,7},{7,6},{8,9},{9,8},{10,11... | collective-permute-start | bytes 1572872 | tf_op jit(solution)/shard_map/gather_saved_block1/ppermute | solution.py:54
  5.9 1.5 %collective-permute-start.2 = (bf16[128,2048]{1,0:T(8,128)(2,1)}, bf16[128,2048]{1,0:T(8,128)(2,1)S(1)}, u32[]{:S(2)}, u32[]{:S(2)}) collective-permute-start(bf16[128,2048]{1,0:T(8,128)(2,1)} %get-tuple-element.43.refs_0_), channel_id=1, source_target_pairs={{0,2},{1,3},{2,0},{3,1},{4,6},{5,7},{6,4},{7,5},{8,10},{9,11},{10,... | collective-permute-start | bytes 1572872 | tf_op jit(solution)/shard_map/gather_saved_block2/ppermute | solution.py:54
  7.4 1.1 %copy-done.3 = bf16[128,2048]{1,0:T(8,128)(2,1)S(1)} copy-done((bf16[128,2048]{1,0:T(8,128)(2,1)S(1)}, bf16[128,2048]{1,0:T(8,128)(2,1)}, u32[]{:S(2)}) %copy-start.3) | copy-done | bytes 524312
  8.5 1.2 %copy-done.7 = f32[1,128,2048]{2,1,0:T(8,128)S(1)} copy-done((f32[1,128,2048]{2,1,0:T(8,128)S(1)}, f32[1,128,2048]{2,1,0:T(8,128)}, u32[]{:S(2)}) %copy-start.7) | copy-done | bytes 1048600
  9.7 0.8 cast.1.refs_2_.refs_0_
  10.6 0.5 collective-permute-start.1
  11.2 0.9 norm.2
  12.1 0.7 copy-done.10
  12.9 6.0 %collective-permute-done.3.refs_1_ = bf16[128,2048]{1,0:T(8,128)(2,1)S(1)} collective-permute-done((bf16[128,2048]{1,0:T(8,128)(2,1)}, bf16[128,2048]{1,0:T(8,128)(2,1)S(1)}, u32[]{:S(2)}, u32[]{:S(2)}) %collective-permute-start.3) | collective-permute-done | bytes 524320 | tf_op jit(solution)/shard_map/gather_saved_block1/ppermute | solution.py:54
  18.9 2.1 %collective-permute-done.2.refs_0_.refs_2_ = bf16[128,2048]{1,0:T(8,128)(2,1)S(1)} collective-permute-done((bf16[128,2048]{1,0:T(8,128)(2,1)}, bf16[128,2048]{1,0:T(8,128)(2,1)S(1)}, u32[]{:S(2)}, u32[]{:S(2)}) %collective-permute-start.2) | collective-permute-done | bytes 524320 | tf_op jit(solution)/shard_map/gather_saved_block2/ppermute | solution.py:54
  21.2 2.0 %collective-permute-start.5 = (bf16[64,2048]{1,0:T(8,128)(2,1)S(1)}, bf16[64,2048]{1,0:T(8,128)(2,1)S(1)}, u32[]{:S(2)}, u32[]{:S(2)}) collective-permute-start(bf16[64,2048]{1,0:T(8,128)(2,1)S(1)} %get-tuple-element.45.refs_5_), channel_id=1, source_target_pairs={{0,2},{1,3},{2,0},{3,1},{4,6},{5,7},{6,4},{7,5},{8,10},{9,11},{10,... | collective-permute-start | bytes 786440 | tf_op jit(solution)/shard_map/gather_saved_block3_row64/ppermute | solution.py:54
  23.2 7.1 %collective-permute-done.1.refs_3_.refs_1_ = bf16[128,2048]{1,0:T(8,128)(2,1)} collective-permute-done((bf16[128,2048]{1,0:T(8,128)(2,1)}, bf16[128,2048]{1,0:T(8,128)(2,1)}, u32[]{:S(2)}, u32[]{:S(2)}) %collective-permute-start.1) | collective-permute-done | bytes 524320 | tf_op jit(solution)/shard_map/gather_grad_block1/ppermute | solution.py:54
  30.2 2.1 %collective-permute-done.refs_2_ = bf16[128,2048]{1,0:T(8,128)(2,1)} collective-permute-done((bf16[128,2048]{1,0:T(8,128)(2,1)}, bf16[128,2048]{1,0:T(8,128)(2,1)}, u32[]{:S(2)}, u32[]{:S(2)}) %collective-permute-start) | collective-permute-done | bytes 524320 | tf_op jit(solution)/shard_map/gather_grad_block2/ppermute | solution.py:54
  32.3 0.9 copy-done.11
  33.3 1.2 %pick.5 = (bf16[64,2048]{1,0:T(8,128)(2,1)S(1)}, bf16[64,2048]{1,0:T(8,128)(2,1)S(1)}, bf16[64,2048]{1,0:T(8,128)(2,1)S(1)}, bf16[64,2048]{1,0:T(8,128)(2,1)S(1)}) custom-call(bf16[64,2048]{1,0:T(8,128)(2,1)S(1)} %get-tuple-element.41.refs_0_, bf16[64,2048]{1,0:T(8,128)(2,1)S(1)} %copy-done.11, bf16[128,2048]{1,0:T(8,128)(2,1)} %collective-permute-done.refs_2_, ...), custom_call_target="tpu_custom_call" | custom-call | flops 1 | bytes 1 | tf_op jit(solution)/shard_map/pick/pallas_call | solution.py:198
  34.6 2.0 %collective-permute-start.11 = (bf16[64,2048]{1,0:T(8,128)(2,1)S(1)}, bf16[64,2048]{1,0:T(8,128)(2,1)S(1)}, u32[]{:S(2)}, u32[]{:S(2)}) collective-permute-start(bf16[64,2048]{1,0:T(8,128)(2,1)S(1)} %get-tuple-element.52), channel_id=1, source_target_pairs={{0,2},{1,3},{2,0},{3,1},{4,6},{5,7},{6,4},{7,5},{8,10},{9,11},{10,... | collective-permute-start | bytes 786440 | tf_op jit(solution)/shard_map/gather_grad_block3_row64/ppermute | solution.py:54
  36.6 1.0 fusion
  37.6 0.2 pad_maximum_fusion
  38.0 1.9 %collective-permute-start.7 = (bf16[64,2048]{1,0:T(8,128)(2,1)S(1)}, bf16[64,2048]{1,0:T(8,128)(2,1)S(1)}, u32[]{:S(2)}, u32[]{:S(2)}) collective-permute-start(bf16[64,2048]{1,0:T(8,128)(2,1)S(1)} %get-tuple-element.47.refs_1_), channel_id=1, source_target_pairs={{0,1},{1,0},{2,3},{3,2},{4,5},{5,4},{6,7},{7,6},{8,9},{9,8},{10,11... | collective-permute-start | bytes 786440 | tf_op jit(solution)/shard_map/gather_input_block1_first64/ppermute | solution.py:54
  40.0 3.6 %project.2 = (bf16[512,512]{1,0:T(8,128)(2,1)S(1)}, bf16[512,512]{1,0:T(8,128)(2,1)S(1)}, bf16[512,512]{1,0:T(8,128)(2,1)S(1)}) custom-call(bf16[128,2048]{1,0:T(8,128)(2,1)S(1)} %copy-done.4, bf16[128,2048]{1,0:T(8,128)(2,1)S(1)} %collective-permute-done.3.refs_1_, bf16[128,2048]{1,0:T(8,128)(2,1)S(1)} %collective-permute-done.2.refs_0_.refs_2_, ...), custom_call_target="tpu_custom_call" | custom-call | flops 1 | bytes 1 | tf_op jit(solution)/shard_map/project/pallas_call | solution.py:198
  43.8 1.9 %collective-permute-start.9 = (bf16[64,2048]{1,0:T(8,128)(2,1)S(1)}, bf16[64,2048]{1,0:T(8,128)(2,1)S(1)}, u32[]{:S(2)}, u32[]{:S(2)}) collective-permute-start(bf16[64,2048]{1,0:T(8,128)(2,1)S(1)} %get-tuple-element.50), channel_id=1, source_target_pairs={{0,2},{1,3},{2,0},{3,1},{4,6},{5,7},{6,4},{7,5},{8,10},{9,11},{10,... | collective-permute-start | bytes 786440 | tf_op jit(solution)/shard_map/gather_input_block2_first64/ppermute | solution.py:54
  45.8 6.8 %backward_heads.1 = (bf16[512,512]{1,0:T(8,128)(2,1)S(1)}, bf16[512,512]{1,0:T(8,128)(2,1)S(1)}, bf16[512,512]{1,0:T(8,128)(2,1)S(1)}) custom-call(bf16[128,2048]{1,0:T(8,128)(2,1)} %cast.1.refs_2_.refs_0_, bf16[128,2048]{1,0:T(8,128)(2,1)} %collective-permute-done.1.refs_3_.refs_1_, bf16[128,2048]{1,0:T(8,128)(2,1)} %collective-permute-done.refs_2_, ...), custom_call_target="tpu_custom_call" | custom-call | flops 8000000000 | bytes 1 | tf_op jit(solution)/shard_map/backward_heads/pallas_call | solution.py:198
  52.6 1.6 %collective-permute-start.12 = (bf16[64,2048]{1,0:T(8,128)(2,1)S(1)}, bf16[64,2048]{1,0:T(8,128)(2,1)S(1)}, u32[]{:S(2)}, u32[]{:S(2)}) collective-permute-start(bf16[64,2048]{1,0:T(8,128)(2,1)S(1)} %get-tuple-element.56.refs_6_), channel_id=1, source_target_pairs={{0,1},{1,0},{2,3},{3,2},{4,5},{5,4},{6,7},{7,6},{8,9},{9,8},{10,11... | collective-permute-start | bytes 786440 | tf_op jit(solution)/shard_map/gather_input_block3_row0/ppermute | solution.py:54
  54.2 0.5 collective-permute-start.13
  54.7 3.4 %backward_terms.1 = (f32[128,2048]{1,0:T(8,128)S(1)}, bf16[128,2048]{1,0:T(8,128)(2,1)S(1)}, bf16[128,2048]{1,0:T(8,128)(2,1)S(1)}, f32[64,2048]{1,0:T(8,128)S(1)}, f32[64,2048]{1,0:T(8,128)S(1)}) custom-call(bf16[512,512]{1,0:T(8,128)(2,1)S(1)} %get-tuple-element.55.refs_2_.refs_0_, bf16[512,512]{1,0:T(8,128)(2,1)S(1)} %get-tuple-element.66.refs_1_, ...), custom_call_target="tpu_custom_call" | custom-call | flops 3000000000 | bytes 1 | tf_op jit(solution)/shard_map/backward_terms/pallas_call | solution.py:198
  58.2 0.2 collective-permute-start.17
  58.4 1.9 %collective-permute-start.18 = (bf16[128,2048]{1,0:T(8,128)(2,1)S(1)}, bf16[128,2048]{1,0:T(8,128)(2,1)S(1)}, u32[]{:S(2)}, u32[]{:S(2)}) collective-permute-start(bf16[128,2048]{1,0:T(8,128)(2,1)S(1)} %get-tuple-element.71), channel_id=1, source_target_pairs={{0,2},{1,3},{2,0},{3,1},{4,6},{5,7},{6,4},{7,5},{8,10},{9,11},{10,... | collective-permute-start | bytes 1572872 | tf_op jit(solution)/shard_map/scatter_grad_block3_part1/ppermute | solution.py:54
  60.3 1.5 %collective-permute-done.12.refs_6_ = bf16[64,2048]{1,0:T(8,128)(2,1)S(1)} collective-permute-done((bf16[64,2048]{1,0:T(8,128)(2,1)S(1)}, bf16[64,2048]{1,0:T(8,128)(2,1)S(1)}, u32[]{:S(2)}, u32[]{:S(2)}) %collective-permute-start.12) | collective-permute-done | bytes 262176 | tf_op jit(solution)/shard_map/gather_input_block3_row0/ppermute | solution.py:54
  61.8 1.6 %collective-permute-done.13.refs_7_ = bf16[64,2048]{1,0:T(8,128)(2,1)S(1)} collective-permute-done((bf16[64,2048]{1,0:T(8,128)(2,1)S(1)}, bf16[64,2048]{1,0:T(8,128)(2,1)S(1)}, u32[]{:S(2)}, u32[]{:S(2)}) %collective-permute-start.13) | collective-permute-done | bytes 262176 | tf_op jit(solution)/shard_map/gather_input_block3_row64/ppermute | solution.py:54
  63.4 3.8 %project.3 = (bf16[512,512]{1,0:T(8,128)(2,1)S(1)}, bf16[512,512]{1,0:T(8,128)(2,1)S(1)}, bf16[512,512]{1,0:T(8,128)(2,1)S(1)}) custom-call(bf16[64,2048]{1,0:T(8,128)(2,1)S(1)} %get-tuple-element.46.refs_0_, bf16[64,2048]{1,0:T(8,128)(2,1)S(1)} %get-tuple-element.47.refs_1_, bf16[64,2048]{1,0:T(8,128)(2,1)S(1)} %collective-permute-done.6.refs_2_, ...), custom_call_target="tpu_custom_call" | custom-call | flops 5000000000 | bytes 1 | tf_op jit(solution)/shard_map/project/pallas_call | solution.py:198
  67.3 2.8 %forward_terms.1 = (bf16[128,2048]{1,0:T(8,128)(2,1)S(1)}, bf16[64,2048]{1,0:T(8,128)(2,1)S(1)}, bf16[64,2048]{1,0:T(8,128)(2,1)S(1)}, f32[128,2048]{1,0:T(8,128)S(1)}, f32[128,2048]{1,0:T(8,128)S(1)}) custom-call(bf16[512,512]{1,0:T(8,128)(2,1)S(1)} %get-tuple-element.58.refs_0_, bf16[512,512]{1,0:T(8,128)(2,1)S(1)} %get-tuple-element.59.refs_1_, ...), custom_call_target="tpu_custom_call" | custom-call | flops 5000000000 | bytes 1 | tf_op jit(solution)/shard_map/forward_terms/pallas_call | solution.py:198
  70.1 0.5 collective-permute-start.16
  70.7 1.9 %collective-permute-done.17.refs_2_.refs_0_ = bf16[128,2048]{1,0:T(8,128)(2,1)S(1)} collective-permute-done((bf16[128,2048]{1,0:T(8,128)(2,1)S(1)}, bf16[128,2048]{1,0:T(8,128)(2,1)S(1)}, u32[]{:S(2)}, u32[]{:S(2)}) %collective-permute-start.17) | collective-permute-done | bytes 524320 | tf_op jit(solution)/shard_map/scatter_grad_block3_part0/ppermute | solution.py:54
  72.6 0.4 collective-permute-done.18.refs_3_
  73.1 1.5 %collective-permute-start.22 = (bf16[64,2048]{1,0:T(8,128)(2,1)S(1)}, bf16[64,2048]{1,0:T(8,128)(2,1)S(1)}, u32[]{:S(2)}, u32[]{:S(2)}) collective-permute-start(bf16[64,2048]{1,0:T(8,128)(2,1)S(1)} %get-tuple-element.72.refs_4_), channel_id=1, source_target_pairs={{0,2},{1,3},{2,0},{3,1},{4,6},{5,7},{6,4},{7,5},{8,10},{9,11},{10,... | collective-permute-start | bytes 786440 | tf_op jit(solution)/shard_map/scatter_grad_block2_part0/ppermute | solution.py:54
  74.6 0.8 collective-permute-start.21
  75.4 2.2 %collective-permute-done.16.refs_3_ = bf16[64,2048]{1,0:T(8,128)(2,1)S(1)} collective-permute-done((bf16[64,2048]{1,0:T(8,128)(2,1)S(1)}, bf16[64,2048]{1,0:T(8,128)(2,1)S(1)}, u32[]{:S(2)}, u32[]{:S(2)}) %collective-permute-start.16) | collective-permute-done | bytes 262176 | tf_op jit(solution)/shard_map/scatter_branch_block3_part1/ppermute | solution.py:54
  77.9 2.5 %collective-permute-start.20 = (bf16[128,2048]{1,0:T(8,128)(2,1)S(1)}, bf16[128,2048]{1,0:T(8,128)(2,1)S(1)}, u32[]{:S(2)}, u32[]{:S(2)}) collective-permute-start(bf16[128,2048]{1,0:T(8,128)(2,1)S(1)} %get-tuple-element.75.refs_6_), channel_id=1, source_target_pairs={{0,5},{1,4},{2,7},{3,6},{4,9},{5,8},{6,11},{7,10},{8,13},{9,12},{1... | collective-permute-start | bytes 1572872 | tf_op jit(solution)/shard_map/scatter_branch_block1_part0/ppermute | solution.py:64
  80.4 0.7 collective-permute-done.14.base_ref.refs_4_
  81.1 1.1 %collective-permute-done.22.refs_2_ = bf16[64,2048]{1,0:T(8,128)(2,1)S(1)} collective-permute-done((bf16[64,2048]{1,0:T(8,128)(2,1)S(1)}, bf16[64,2048]{1,0:T(8,128)(2,1)S(1)}, u32[]{:S(2)}, u32[]{:S(2)}) %collective-permute-start.22) | collective-permute-done | bytes 262176 | tf_op jit(solution)/shard_map/scatter_grad_block2_part0/ppermute | solution.py:54
  82.2 0.4 collective-permute-done.21.refs_1_
  82.6 0.6 input_grad.1
  83.1 1.9 %collective-permute-start.23 = (bf16[128,2048]{1,0:T(8,128)(2,1)S(1)}, bf16[128,2048]{1,0:T(8,128)(2,1)S(1)}, u32[]{:S(2)}, u32[]{:S(2)}) collective-permute-start(bf16[128,2048]{1,0:T(8,128)(2,1)S(1)} %input_grad.1), channel_id=1, source_target_pairs={{0,28},{4,0},{8,4},{12,8},{16,12},{20,16},{24,20},{28,24},{1,29},{... | collective-permute-start | bytes 1572872 | tf_op jit(solution)/shard_map/ppermute | solution.py:70
  85.1 6.6 %collective-permute-done.19.refs_0_.refs_1_ = bf16[128,2048]{1,0:T(8,128)(2,1)S(1)} collective-permute-done((bf16[128,2048]{1,0:T(8,128)(2,1)S(1)}, bf16[128,2048]{1,0:T(8,128)(2,1)S(1)}, u32[]{:S(2)}, u32[]{:S(2)}) %collective-permute-start.19) | collective-permute-done | bytes 524320 | tf_op jit(solution)/shard_map/scatter_branch_block2_part0/ppermute | solution.py:64
  91.6 8.7 %collective-permute-done.20.refs_2_.refs_3_ = bf16[128,2048]{1,0:T(8,128)(2,1)S(1)} collective-permute-done((bf16[128,2048]{1,0:T(8,128)(2,1)S(1)}, bf16[128,2048]{1,0:T(8,128)(2,1)S(1)}, u32[]{:S(2)}, u32[]{:S(2)}) %collective-permute-start.20) | collective-permute-done | bytes 524320 | tf_op jit(solution)/shard_map/scatter_branch_block1_part0/ppermute | solution.py:64
  100.3 1.1 %activation_sum.1 = (f32[1,128,2048]{2,1,0:T(8,128)}, f32[8,128]{1,0:T(8,128)S(1)}) custom-call(bf16[128,2048]{1,0:T(8,128)(2,1)S(1)} %collective-permute-done.14.base_ref.refs_4_, bf16[128,2048]{1,0:T(8,128)(2,1)S(1)} %collective-permute-done.19.refs_0_.refs_1_, bf16[128,2048]{1,0:T(8,128)(2,1)S(1)} %collective-permute-done.19.refs_0_.refs_1_, ...), custom_call_target="tpu_custom_call" | custom-call | flops 8000000000 | bytes 1 | tf_op jit(solution)/shard_map/activation_sum/pallas_call | solution.py:198
  101.5 1.1 %widen.1 = f32[1,128,2048]{2,1,0:T(8,128)} custom-call(bf16[128,2048]{1,0:T(8,128)(2,1)S(1)} %collective-permute-done.23.in_any, f32[8,128]{1,0:T(8,128)S(1)} %get-tuple-element.79.refs_0_), custom_call_target="tpu_custom_call" | custom-call | flops 1 | bytes 1 | tf_op jit(solution)/shard_map/widen/pallas_call | solution.py:198
  (54 shorter events, 1.4 us)
Async XLA Ops:
  0.6 10.6 %copy-start.13 = (f32[1,2048]{1,0:T(1,128)S(1)}, f32[1,2048]{1,0:T(1,128)}, u32[]{:S(2)}) copy-start(f32[1,2048]{1,0:T(1,128)} %gain_ref.1) | copy-start | bytes 24580
  2.9 16.0 %collective-permute-start.3 = (bf16[128,2048]{1,0:T(8,128)(2,1)}, bf16[128,2048]{1,0:T(8,128)(2,1)S(1)}, u32[]{:S(2)}, u32[]{:S(2)}) collective-permute-start(bf16[128,2048]{1,0:T(8,128)(2,1)} %get-tuple-element.43.refs_0_), channel_id=1, source_target_pairs={{0,1},{1,0},{2,3},{3,2},{4,5},{5,4},{6,7},{7,6},{8,9},{9,8},{10,11... | collective-permute-start | bytes 1572872 | tf_op jit(solution)/shard_map/gather_saved_block1/ppermute | solution.py:54
  5.9 15.1 %collective-permute-start.2 = (bf16[128,2048]{1,0:T(8,128)(2,1)}, bf16[128,2048]{1,0:T(8,128)(2,1)S(1)}, u32[]{:S(2)}, u32[]{:S(2)}) collective-permute-start(bf16[128,2048]{1,0:T(8,128)(2,1)} %get-tuple-element.43.refs_0_), channel_id=1, source_target_pairs={{0,2},{1,3},{2,0},{3,1},{4,6},{5,7},{6,4},{7,5},{8,10},{9,11},{10,... | collective-permute-start | bytes 1572872 | tf_op jit(solution)/shard_map/gather_saved_block2/ppermute | solution.py:54
  7.4 1.1 %copy-start.3 = (bf16[128,2048]{1,0:T(8,128)(2,1)S(1)}, bf16[128,2048]{1,0:T(8,128)(2,1)}, u32[]{:S(2)}) copy-start(bf16[128,2048]{1,0:T(8,128)(2,1)} %get-tuple-element.43.refs_0_) | copy-start | bytes 1572868
  8.5 1.2 %copy-start.7 = (f32[1,128,2048]{2,1,0:T(8,128)S(1)}, f32[1,128,2048]{2,1,0:T(8,128)}, u32[]{:S(2)}) copy-start(f32[1,128,2048]{2,1,0:T(8,128)} %param.10) | copy-start | bytes 3145732
  9.7 1.5 %copy-start.5 = (f32[1,128,2048]{2,1,0:T(8,128)S(1)}, f32[1,128,2048]{2,1,0:T(8,128)}, u32[]{:S(2)}) copy-start(f32[1,128,2048]{2,1,0:T(8,128)} %param.8) | copy-start | bytes 3145732
  10.6 19.6 %collective-permute-start.1 = (bf16[128,2048]{1,0:T(8,128)(2,1)}, bf16[128,2048]{1,0:T(8,128)(2,1)}, u32[]{:S(2)}, u32[]{:S(2)}) collective-permute-start(bf16[128,2048]{1,0:T(8,128)(2,1)} %cast.1.refs_2_.refs_0_), channel_id=1, source_target_pairs={{0,1},{1,0},{2,3},{3,2},{4,5},{5,4},{6,7},{7,6},{8,9},{9,8},{10,11... | collective-permute-start | bytes 1572872 | tf_op jit(solution)/shard_map/gather_grad_block1/ppermute | solution.py:54
  11.1 21.2 %collective-permute-start = (bf16[128,2048]{1,0:T(8,128)(2,1)}, bf16[128,2048]{1,0:T(8,128)(2,1)}, u32[]{:S(2)}, u32[]{:S(2)}) collective-permute-start(bf16[128,2048]{1,0:T(8,128)(2,1)} %cast.1.refs_2_.refs_0_), channel_id=1, source_target_pairs={{0,2},{1,3},{2,0},{3,1},{4,6},{5,7},{6,4},{7,5},{8,10},{9,11},{10,... | collective-permute-start | bytes 1572872 | tf_op jit(solution)/shard_map/gather_grad_block2/ppermute | solution.py:54
  11.2 28.7 %copy-start.2 = (bf16[1,2048,512]{2,1,0:T(8,128)(2,1)S(1)}, bf16[1,2048,512]{2,1,0:T(8,128)(2,1)}, u32[]{:S(2)}) copy-start(bf16[1,2048,512]{2,1,0:T(8,128)(2,1)} %param.14) | copy-start | bytes 6291460
  12.1 0.7 copy-start.10
  21.0 19.0 %copy-start.4 = (bf16[128,2048]{1,0:T(8,128)(2,1)S(1)}, bf16[128,2048]{1,0:T(8,128)(2,1)}, u32[]{:S(2)}) copy-start(bf16[128,2048]{1,0:T(8,128)(2,1)} %get-tuple-element.43.refs_0_) | copy-start | bytes 1572868
  21.0 16.9 %collective-permute-start.4 = (bf16[64,2048]{1,0:T(8,128)(2,1)S(1)}, bf16[64,2048]{1,0:T(8,128)(2,1)S(1)}, u32[]{:S(2)}, u32[]{:S(2)}) collective-permute-start(bf16[64,2048]{1,0:T(8,128)(2,1)S(1)} %get-tuple-element.44.refs_4_), channel_id=1, source_target_pairs={{0,1},{1,0},{2,3},{3,2},{4,5},{5,4},{6,7},{7,6},{8,9},{9,8},{10,11... | collective-permute-start | bytes 786440 | tf_op jit(solution)/shard_map/gather_saved_block3_row0/ppermute | solution.py:54
  21.2 18.8 %collective-permute-start.5 = (bf16[64,2048]{1,0:T(8,128)(2,1)S(1)}, bf16[64,2048]{1,0:T(8,128)(2,1)S(1)}, u32[]{:S(2)}, u32[]{:S(2)}) collective-permute-start(bf16[64,2048]{1,0:T(8,128)(2,1)S(1)} %get-tuple-element.45.refs_5_), channel_id=1, source_target_pairs={{0,2},{1,3},{2,0},{3,1},{4,6},{5,7},{6,4},{7,5},{8,10},{9,11},{10,... | collective-permute-start | bytes 786440 | tf_op jit(solution)/shard_map/gather_saved_block3_row64/ppermute | solution.py:54
  32.3 1.0 copy-start.11
  33.3 6.7 %copy-start = (bf16[1,2048,512]{2,1,0:T(8,128)(2,1)S(1)}, bf16[1,2048,512]{2,1,0:T(8,128)(2,1)}, u32[]{:S(2)}) copy-start(bf16[1,2048,512]{2,1,0:T(8,128)(2,1)} %param.12) | copy-start | bytes 6291460
  33.3 6.7 %copy-start.1 = (bf16[1,2048,512]{2,1,0:T(8,128)(2,1)S(1)}, bf16[1,2048,512]{2,1,0:T(8,128)(2,1)}, u32[]{:S(2)}) copy-start(bf16[1,2048,512]{2,1,0:T(8,128)(2,1)} %param.13) | copy-start | bytes 6291460
  34.5 9.3 %collective-permute-start.10 = (bf16[64,2048]{1,0:T(8,128)(2,1)S(1)}, bf16[64,2048]{1,0:T(8,128)(2,1)S(1)}, u32[]{:S(2)}, u32[]{:S(2)}) collective-permute-start(bf16[64,2048]{1,0:T(8,128)(2,1)S(1)} %get-tuple-element.51), channel_id=1, source_target_pairs={{0,1},{1,0},{2,3},{3,2},{4,5},{5,4},{6,7},{7,6},{8,9},{9,8},{10,11... | collective-permute-start | bytes 786440 | tf_op jit(solution)/shard_map/gather_grad_block3_row0/ppermute | solution.py:54
  34.6 11.1 %collective-permute-start.11 = (bf16[64,2048]{1,0:T(8,128)(2,1)S(1)}, bf16[64,2048]{1,0:T(8,128)(2,1)S(1)}, u32[]{:S(2)}, u32[]{:S(2)}) collective-permute-start(bf16[64,2048]{1,0:T(8,128)(2,1)S(1)} %get-tuple-element.52), channel_id=1, source_target_pairs={{0,2},{1,3},{2,0},{3,1},{4,6},{5,7},{6,4},{7,5},{8,10},{9,11},{10,... | collective-permute-start | bytes 786440 | tf_op jit(solution)/shard_map/gather_grad_block3_row64/ppermute | solution.py:54
  37.8 14.7 %collective-permute-start.8 = (bf16[64,2048]{1,0:T(8,128)(2,1)S(1)}, bf16[64,2048]{1,0:T(8,128)(2,1)S(1)}, u32[]{:S(2)}, u32[]{:S(2)}) collective-permute-start(bf16[64,2048]{1,0:T(8,128)(2,1)S(1)} %get-tuple-element.46.refs_0_), channel_id=1, source_target_pairs={{0,2},{1,3},{2,0},{3,1},{4,6},{5,7},{6,4},{7,5},{8,10},{9,11},{10,... | collective-permute-start | bytes 786440 | tf_op jit(solution)/shard_map/gather_input_block2_first0/ppermute | solution.py:54
  38.0 14.6 %collective-permute-start.7 = (bf16[64,2048]{1,0:T(8,128)(2,1)S(1)}, bf16[64,2048]{1,0:T(8,128)(2,1)S(1)}, u32[]{:S(2)}, u32[]{:S(2)}) collective-permute-start(bf16[64,2048]{1,0:T(8,128)(2,1)S(1)} %get-tuple-element.47.refs_1_), channel_id=1, source_target_pairs={{0,1},{1,0},{2,3},{3,2},{4,5},{5,4},{6,7},{7,6},{8,9},{9,8},{10,11... | collective-permute-start | bytes 786440 | tf_op jit(solution)/shard_map/gather_input_block1_first64/ppermute | solution.py:54
  39.9 3.6 %copy-start.12 = (bf16[64,2048]{1,0:T(8,128)(2,1)S(1)}, bf16[64,2048]{1,0:T(8,128)(2,1)}, u32[]{:S(2)}) copy-start(bf16[64,2048]{1,0:T(8,128)(2,1)} %copy-done.10) | copy-start | bytes 786436
  40.0 5.8 %copy-start.14 = (bf16[1,2048,512]{2,1,0:T(8,128)(2,1)S(1)}, bf16[1,2048,512]{2,1,0:T(8,128)(2,1)}, u32[]{:S(2)}) copy-start(bf16[1,2048,512]{2,1,0:T(8,128)(2,1)} %param.15) | copy-start | bytes 6291460
  43.7 14.7 %collective-permute-start.6 = (bf16[64,2048]{1,0:T(8,128)(2,1)S(1)}, bf16[64,2048]{1,0:T(8,128)(2,1)S(1)}, u32[]{:S(2)}, u32[]{:S(2)}) collective-permute-start(bf16[64,2048]{1,0:T(8,128)(2,1)S(1)} %get-tuple-element.49), channel_id=1, source_target_pairs={{0,1},{1,0},{2,3},{3,2},{4,5},{5,4},{6,7},{7,6},{8,9},{9,8},{10,11... | collective-permute-start | bytes 786440 | tf_op jit(solution)/shard_map/gather_input_block1_first0/ppermute | solution.py:54
  43.8 16.4 %collective-permute-start.9 = (bf16[64,2048]{1,0:T(8,128)(2,1)S(1)}, bf16[64,2048]{1,0:T(8,128)(2,1)S(1)}, u32[]{:S(2)}, u32[]{:S(2)}) collective-permute-start(bf16[64,2048]{1,0:T(8,128)(2,1)S(1)} %get-tuple-element.50), channel_id=1, source_target_pairs={{0,2},{1,3},{2,0},{3,1},{4,6},{5,7},{6,4},{7,5},{8,10},{9,11},{10,... | collective-permute-start | bytes 786440 | tf_op jit(solution)/shard_map/gather_input_block2_first64/ppermute | solution.py:54
  52.6 9.2 %collective-permute-start.12 = (bf16[64,2048]{1,0:T(8,128)(2,1)S(1)}, bf16[64,2048]{1,0:T(8,128)(2,1)S(1)}, u32[]{:S(2)}, u32[]{:S(2)}) collective-permute-start(bf16[64,2048]{1,0:T(8,128)(2,1)S(1)} %get-tuple-element.56.refs_6_), channel_id=1, source_target_pairs={{0,1},{1,0},{2,3},{3,2},{4,5},{5,4},{6,7},{7,6},{8,9},{9,8},{10,11... | collective-permute-start | bytes 786440 | tf_op jit(solution)/shard_map/gather_input_block3_row0/ppermute | solution.py:54
  54.2 9.2 %collective-permute-start.13 = (bf16[64,2048]{1,0:T(8,128)(2,1)S(1)}, bf16[64,2048]{1,0:T(8,128)(2,1)S(1)}, u32[]{:S(2)}, u32[]{:S(2)}) collective-permute-start(bf16[64,2048]{1,0:T(8,128)(2,1)S(1)} %get-tuple-element.57.refs_7_), channel_id=1, source_target_pairs={{0,2},{1,3},{2,0},{3,1},{4,6},{5,7},{6,4},{7,5},{8,10},{9,11},{10,... | collective-permute-start | bytes 786440 | tf_op jit(solution)/shard_map/gather_input_block3_row64/ppermute | solution.py:54
  58.2 14.4 %collective-permute-start.17 = (bf16[128,2048]{1,0:T(8,128)(2,1)S(1)}, bf16[128,2048]{1,0:T(8,128)(2,1)S(1)}, u32[]{:S(2)}, u32[]{:S(2)}) collective-permute-start(bf16[128,2048]{1,0:T(8,128)(2,1)S(1)} %get-tuple-element.70), channel_id=1, source_target_pairs={{0,1},{1,0},{2,3},{3,2},{4,5},{5,4},{6,7},{7,6},{8,9},{9,8},{10,11... | collective-permute-start | bytes 1572872 | tf_op jit(solution)/shard_map/scatter_grad_block3_part0/ppermute | solution.py:54
  58.3 8.9 %copy-start.6 = (f32[1,128,2048]{2,1,0:T(8,128)S(1)}, f32[1,128,2048]{2,1,0:T(8,128)}, u32[]{:S(2)}) copy-start(f32[1,128,2048]{2,1,0:T(8,128)} %param.8) | copy-start | bytes 3145732
  58.4 14.7 %collective-permute-start.18 = (bf16[128,2048]{1,0:T(8,128)(2,1)S(1)}, bf16[128,2048]{1,0:T(8,128)(2,1)S(1)}, u32[]{:S(2)}, u32[]{:S(2)}) collective-permute-start(bf16[128,2048]{1,0:T(8,128)(2,1)S(1)} %get-tuple-element.71), channel_id=1, source_target_pairs={{0,2},{1,3},{2,0},{3,1},{4,6},{5,7},{6,4},{7,5},{8,10},{9,11},{10,... | collective-permute-start | bytes 1572872 | tf_op jit(solution)/shard_map/scatter_grad_block3_part1/ppermute | solution.py:54
  70.1 7.5 %collective-permute-start.16 = (bf16[64,2048]{1,0:T(8,128)(2,1)S(1)}, bf16[64,2048]{1,0:T(8,128)(2,1)S(1)}, u32[]{:S(2)}, u32[]{:S(2)}) collective-permute-start(bf16[64,2048]{1,0:T(8,128)(2,1)S(1)} %get-tuple-element.65), channel_id=1, source_target_pairs={{0,2},{1,3},{2,0},{3,1},{4,6},{5,7},{6,4},{7,5},{8,10},{9,11},{10,... | collective-permute-start | bytes 786440 | tf_op jit(solution)/shard_map/scatter_branch_block3_part1/ppermute | solution.py:54
  70.6 7.1 %collective-permute-start.15 = (bf16[64,2048]{1,0:T(8,128)(2,1)S(1)}, bf16[64,2048]{1,0:T(8,128)(2,1)S(1)}, u32[]{:S(2)}, u32[]{:S(2)}) collective-permute-start(bf16[64,2048]{1,0:T(8,128)(2,1)S(1)} %get-tuple-element.64.refs_4_), channel_id=1, source_target_pairs={{0,1},{1,0},{2,3},{3,2},{4,5},{5,4},{6,7},{7,6},{8,9},{9,8},{10,11... | collective-permute-start | bytes 786440 | tf_op jit(solution)/shard_map/scatter_branch_block3_part0/ppermute | solution.py:54
  70.7 10.4 %collective-permute-start.14 = (bf16[128,2048]{1,0:T(8,128)(2,1)S(1)}, bf16[128,2048]{1,0:T(8,128)(2,1)S(1)}, u32[]{:S(2)}, u32[]{:S(2)}) collective-permute-start(bf16[128,2048]{1,0:T(8,128)(2,1)S(1)} %get-tuple-element.61), channel_id=1, source_target_pairs={{0,4},{1,5},{2,6},{3,7},{4,8},{5,9},{6,10},{7,11},{8,12},{9,13},{1... | collective-permute-start | bytes 1572872 | tf_op jit(solution)/shard_map/ppermute | solution.py:64
  73.1 9.0 %collective-permute-start.22 = (bf16[64,2048]{1,0:T(8,128)(2,1)S(1)}, bf16[64,2048]{1,0:T(8,128)(2,1)S(1)}, u32[]{:S(2)}, u32[]{:S(2)}) collective-permute-start(bf16[64,2048]{1,0:T(8,128)(2,1)S(1)} %get-tuple-element.72.refs_4_), channel_id=1, source_target_pairs={{0,2},{1,3},{2,0},{3,1},{4,6},{5,7},{6,4},{7,5},{8,10},{9,11},{10,... | collective-permute-start | bytes 786440 | tf_op jit(solution)/shard_map/scatter_grad_block2_part0/ppermute | solution.py:54
  74.6 7.9 %collective-permute-start.21 = (bf16[64,2048]{1,0:T(8,128)(2,1)S(1)}, bf16[64,2048]{1,0:T(8,128)(2,1)S(1)}, u32[]{:S(2)}, u32[]{:S(2)}) collective-permute-start(bf16[64,2048]{1,0:T(8,128)(2,1)S(1)} %get-tuple-element.73.refs_5_), channel_id=1, source_target_pairs={{0,1},{1,0},{2,3},{3,2},{4,5},{5,4},{6,7},{7,6},{8,9},{9,8},{10,11... | collective-permute-start | bytes 786440 | tf_op jit(solution)/shard_map/scatter_grad_block1_part1/ppermute | solution.py:54
  77.6 4.9 %copy-start.8 = (f32[1,128,2048]{2,1,0:T(8,128)S(1)}, f32[1,128,2048]{2,1,0:T(8,128)}, u32[]{:S(2)}) copy-start(f32[1,128,2048]{2,1,0:T(8,128)} %param.10) | copy-start | bytes 3145732
  77.6 4.9 %copy-start.9 = (f32[1,128,2048]{2,1,0:T(8,128)S(1)}, f32[1,128,2048]{2,1,0:T(8,128)}, u32[]{:S(2)}) copy-start(f32[1,128,2048]{2,1,0:T(8,128)} %param.9) | copy-start | bytes 3145732
  77.6 4.9 %copy-start.15 = (f32[128,1]{1,0:T(8,128)S(1)}, f32[128,1]{1,0:T(8,128)}, u32[]{:S(2)}) copy-start(f32[128,1]{1,0:T(8,128)} %get-tuple-element.78.inv_ref) | copy-start | bytes 1540
  77.8 13.8 %collective-permute-start.19 = (bf16[128,2048]{1,0:T(8,128)(2,1)S(1)}, bf16[128,2048]{1,0:T(8,128)(2,1)S(1)}, u32[]{:S(2)}, u32[]{:S(2)}) collective-permute-start(bf16[128,2048]{1,0:T(8,128)(2,1)S(1)} %get-tuple-element.74.refs_5_), channel_id=1, source_target_pairs={{0,6},{1,7},{2,4},{3,5},{4,10},{5,11},{6,8},{7,9},{8,14},{9,15},{1... | collective-permute-start | bytes 1572872 | tf_op jit(solution)/shard_map/scatter_branch_block2_part0/ppermute | solution.py:64
  77.9 22.5 %collective-permute-start.20 = (bf16[128,2048]{1,0:T(8,128)(2,1)S(1)}, bf16[128,2048]{1,0:T(8,128)(2,1)S(1)}, u32[]{:S(2)}, u32[]{:S(2)}) collective-permute-start(bf16[128,2048]{1,0:T(8,128)(2,1)S(1)} %get-tuple-element.75.refs_6_), channel_id=1, source_target_pairs={{0,5},{1,4},{2,7},{3,6},{4,9},{5,8},{6,11},{7,10},{8,13},{9,12},{1... | collective-permute-start | bytes 1572872 | tf_op jit(solution)/shard_map/scatter_branch_block1_part0/ppermute | solution.py:64
  83.1 18.4 %collective-permute-start.23 = (bf16[128,2048]{1,0:T(8,128)(2,1)S(1)}, bf16[128,2048]{1,0:T(8,128)(2,1)S(1)}, u32[]{:S(2)}, u32[]{:S(2)}) collective-permute-start(bf16[128,2048]{1,0:T(8,128)(2,1)S(1)} %input_grad.1), channel_id=1, source_target_pairs={{0,28},{4,0},{8,4},{12,8},{16,12},{20,16},{24,20},{28,24},{1,29},{... | collective-permute-start | bytes 1572872 | tf_op jit(solution)/shard_map/ppermute | solution.py:70
where the time goes:
time: 104 us; the launch traced here: 103 us
  waiting for transfers between devices  42.4 us (41%)
  Pallas kernels  28.9 us (28%)
  starting transfers between devices  25.2 us (24%)
  local copies, waits for them, and re-layouts  3.99 us (4%)
  other arithmetic  1.28 us (1%)
  between operations  1.04 us (1%)
    pallas_call x17, Pallas kernels, call(): pl.pallas_call(kernel, out_shape=out_shapes, in_specs=in_specs, out_specs...  28.9 us
    ppermute x20, waiting for transfers between devices, across(): return lax.ppermute(value, 'seq', [(i, i ^ 1 << bit) for i in range(count)])  26.4 us
    ppermute x20, starting transfers between devices, across(): return lax.ppermute(value, 'seq', [(i, i ^ 1 << bit) for i in range(count)])  20.6 us
    ppermute x3, waiting for transfers between devices, across_and_on(): return lax.ppermute(value, ('pipe', 'seq'), pairs)  16 us
    unnamed x32, local copies, waits for them, and re-layouts  3.99 us
    ppermute x3, starting transfers between devices, across_and_on(): return lax.ppermute(value, ('pipe', 'seq'), pairs)  2.6 us
  transfers between devices with their start and end apart: 24, of which 14 were waited for; matrix products, arithmetic and copies ran while one was open for 1% of the time, Pallas kernels for 25%

commit v1 on v0

--- a/solution.py
+++ b/solution.py
@@ -648,7 +648,7 @@
     whole = [(0, rows)]
     projections = (own_query, own_key, own_value)
     (normed_bwd,), inv_bwd = normed_rows(saved_in, gain, whole, vmem=62)
-    grad_low = cast_rows(grad, [normed_bwd])
+    grad_low = cast_rows(grad, [normed_bwd, cosine, sine])
     all_bwd = gather_first(normed_bwd, "saved")
     all_grad = gather_first(grad_low, "grad")
     normed_fwd, _ = normed_rows(act_in, gain, bounds)

time: 104 us -> 103 us (level)
  waiting for transfers between devices: 42.4 us -> 47.5 us
  local copies, waits for them, and re-layouts: 3.99 us -> 0.06 us
  Pallas kernels: 28.9 us -> 25.9 us
  starting transfers between devices: 25.2 us -> 26.8 us
    ppermute x20, waiting for transfers between devices: 26.4 us -> 31.2 us  [across(): return lax.ppermute(value, 'seq', [(i, i ^ 1 << bit) for i in range(count)])]
    unnamed x32 -> x20, local copies, waits for them, and re-layouts: 3.99 us -> 0.06 us
    pallas_call x17, Pallas kernels: 28.9 us -> 25.9 us  [call(): pl.pallas_call(kernel, out_shape=out_shapes, in_specs=in_specs, out_specs...]
    ppermute x20, starting transfers between devices: 20.6 us -> 22.1 us  [across(): return lax.ppermute(value, 'seq', [(i, i ^ 1 << bit) for i in range(count)])]
  transfers between devices with their start and end apart: 24 -> 24, of which waited for: 14 -> 13; matrix products, arithmetic and copies ran while one was open for 1% -> 1% of each run, Pallas kernels for 25% -> 22%
where the time goes in v1:
time: 103 us
  waiting for transfers between devices  47.5 us (46%)
  starting transfers between devices  26.8 us (26%)
  Pallas kernels  25.9 us (25%)
  other arithmetic  1.29 us (1%)
  between operations  1.05 us (1%)
    ppermute x20, waiting for transfers between devices, across(): return lax.ppermute(value, 'seq', [(i, i ^ 1 << bit) for i in range(count)])  31.2 us
    pallas_call x17, Pallas kernels, call(): pl.pallas_call(kernel, out_shape=out_shapes, in_specs=in_specs, out_specs...  25.9 us
    ppermute x20, starting transfers between devices, across(): return lax.ppermute(value, 'seq', [(i, i ^ 1 << bit) for i in range(count)])  22.1 us
    ppermute x3, waiting for transfers between devices, across_and_on(): return lax.ppermute(value, ('pipe', 'seq'), pairs)  16.3 us
    ppermute x3, starting transfers between devices, across_and_on(): return lax.ppermute(value, ('pipe', 'seq'), pairs)  2.83 us
  transfers between devices with their start and end apart: 24, of which 13 were waited for; matrix products, arithmetic and copies ran while one was open for 1% of the time, Pallas kernels for 22%

profile of v1, /device:TPU:0, one launch (start us, length us, event | category | flops | bytes accessed | tf_op | source)
XLA Modules:
  0.0 102.6 jit_solution(7152268035263405723)
XLA Ops:
  0.6 2.3 %norm.3 = (bf16[128,2048]{1,0:T(8,128)(2,1)}, f32[128,1]{1,0:T(8,128)}) custom-call(f32[128,2048]{1,0:T(8,128)} %bitcast.22, f32[1,2048]{1,0:T(1,128)} %gain_ref.1), custom_call_target="tpu_custom_call" | custom-call | flops 1 | bytes 1 | tf_op jit(solution)/shard_map/norm/pallas_call | solution.py:198
  3.0 3.0 %collective-permute-start.3 = (bf16[128,2048]{1,0:T(8,128)(2,1)}, bf16[128,2048]{1,0:T(8,128)(2,1)S(1)}, u32[]{:S(2)}, u32[]{:S(2)}) collective-permute-start(bf16[128,2048]{1,0:T(8,128)(2,1)} %get-tuple-element.43.refs_0_), channel_id=1, source_target_pairs={{0,1},{1,0},{2,3},{3,2},{4,5},{5,4},{6,7},{7,6},{8,9},{9,8},{10,11... | collective-permute-start | bytes 1572872 | tf_op jit(solution)/shard_map/gather_saved_block1/ppermute | solution.py:54
  6.0 1.5 %collective-permute-start.2 = (bf16[128,2048]{1,0:T(8,128)(2,1)}, bf16[128,2048]{1,0:T(8,128)(2,1)S(1)}, u32[]{:S(2)}, u32[]{:S(2)}) collective-permute-start(bf16[128,2048]{1,0:T(8,128)(2,1)} %get-tuple-element.43.refs_0_), channel_id=1, source_target_pairs={{0,2},{1,3},{2,0},{3,1},{4,6},{5,7},{6,4},{7,5},{8,10},{9,11},{10,... | collective-permute-start | bytes 1572872 | tf_op jit(solution)/shard_map/gather_saved_block2/ppermute | solution.py:54
  7.5 0.1 convert_bitcast_fusion
  7.6 1.0 fusion
  8.6 0.2 pad_maximum_fusion
  9.0 0.6 collective-permute-start.1
  9.6 9.3 %collective-permute-done.3.refs_1_ = bf16[128,2048]{1,0:T(8,128)(2,1)S(1)} collective-permute-done((bf16[128,2048]{1,0:T(8,128)(2,1)}, bf16[128,2048]{1,0:T(8,128)(2,1)S(1)}, u32[]{:S(2)}, u32[]{:S(2)}) %collective-permute-start.3) | collective-permute-done | bytes 524320 | tf_op jit(solution)/shard_map/gather_saved_block1/ppermute | solution.py:54
  19.0 2.1 %collective-permute-done.2.refs_0_.refs_2_ = bf16[128,2048]{1,0:T(8,128)(2,1)S(1)} collective-permute-done((bf16[128,2048]{1,0:T(8,128)(2,1)}, bf16[128,2048]{1,0:T(8,128)(2,1)S(1)}, u32[]{:S(2)}, u32[]{:S(2)}) %collective-permute-start.2) | collective-permute-done | bytes 524320 | tf_op jit(solution)/shard_map/gather_saved_block2/ppermute | solution.py:54
  21.1 0.1 collective-permute-start.4
  21.3 2.0 %collective-permute-start.5 = (bf16[64,2048]{1,0:T(8,128)(2,1)S(1)}, bf16[64,2048]{1,0:T(8,128)(2,1)S(1)}, u32[]{:S(2)}, u32[]{:S(2)}) collective-permute-start(bf16[64,2048]{1,0:T(8,128)(2,1)S(1)} %get-tuple-element.45.refs_5_), channel_id=1, source_target_pairs={{0,2},{1,3},{2,0},{3,1},{4,6},{5,7},{6,4},{7,5},{8,10},{9,11},{10,... | collective-permute-start | bytes 786440 | tf_op jit(solution)/shard_map/gather_saved_block3_row64/ppermute | solution.py:54
  23.3 0.9 norm.2
  24.2 6.0 %collective-permute-done.1.refs_3_.refs_1_ = bf16[128,2048]{1,0:T(8,128)(2,1)S(1)} collective-permute-done((bf16[128,2048]{1,0:T(8,128)(2,1)S(1)}, bf16[128,2048]{1,0:T(8,128)(2,1)S(1)}, u32[]{:S(2)}, u32[]{:S(2)}) %collective-permute-start.1) | collective-permute-done | bytes 524320 | tf_op jit(solution)/shard_map/gather_grad_block1/ppermute | solution.py:54
  30.2 2.1 %collective-permute-done.refs_2_ = bf16[128,2048]{1,0:T(8,128)(2,1)S(1)} collective-permute-done((bf16[128,2048]{1,0:T(8,128)(2,1)S(1)}, bf16[128,2048]{1,0:T(8,128)(2,1)S(1)}, u32[]{:S(2)}, u32[]{:S(2)}) %collective-permute-start) | collective-permute-done | bytes 524320 | tf_op jit(solution)/shard_map/gather_grad_block2/ppermute | solution.py:54
  32.3 0.1 pick.5
  32.4 0.1 collective-permute-start.10
  32.5 2.0 %collective-permute-start.11 = (bf16[64,2048]{1,0:T(8,128)(2,1)S(1)}, bf16[64,2048]{1,0:T(8,128)(2,1)S(1)}, u32[]{:S(2)}, u32[]{:S(2)}) collective-permute-start(bf16[64,2048]{1,0:T(8,128)(2,1)S(1)} %get-tuple-element.52), channel_id=1, source_target_pairs={{0,2},{1,3},{2,0},{3,1},{4,6},{5,7},{6,4},{7,5},{8,10},{9,11},{10,... | collective-permute-start | bytes 786440 | tf_op jit(solution)/shard_map/gather_grad_block3_row64/ppermute | solution.py:54
  34.6 1.2 %collective-permute-done.4.refs_3_ = bf16[64,2048]{1,0:T(8,128)(2,1)S(1)} collective-permute-done((bf16[64,2048]{1,0:T(8,128)(2,1)S(1)}, bf16[64,2048]{1,0:T(8,128)(2,1)S(1)}, u32[]{:S(2)}, u32[]{:S(2)}) %collective-permute-start.4) | collective-permute-done | bytes 262176 | tf_op jit(solution)/shard_map/gather_saved_block3_row0/ppermute | solution.py:54
  35.8 2.1 %collective-permute-start.7 = (bf16[64,2048]{1,0:T(8,128)(2,1)S(1)}, bf16[64,2048]{1,0:T(8,128)(2,1)S(1)}, u32[]{:S(2)}, u32[]{:S(2)}) collective-permute-start(bf16[64,2048]{1,0:T(8,128)(2,1)S(1)} %get-tuple-element.47.refs_1_), channel_id=1, source_target_pairs={{0,1},{1,0},{2,3},{3,2},{4,5},{5,4},{6,7},{7,6},{8,9},{9,8},{10,11... | collective-permute-start | bytes 786440 | tf_op jit(solution)/shard_map/gather_input_block1_first64/ppermute | solution.py:54
  37.9 3.6 %project.2 = (bf16[512,512]{1,0:T(8,128)(2,1)S(1)}, bf16[512,512]{1,0:T(8,128)(2,1)S(1)}, bf16[512,512]{1,0:T(8,128)(2,1)S(1)}) custom-call(bf16[128,2048]{1,0:T(8,128)(2,1)S(1)} %copy-done.3, bf16[128,2048]{1,0:T(8,128)(2,1)S(1)} %collective-permute-done.3.refs_1_, bf16[128,2048]{1,0:T(8,128)(2,1)S(1)} %collective-permute-done.2.refs_0_.refs_2_, ...), custom_call_target="tpu_custom_call" | custom-call | flops 1 | bytes 1 | tf_op jit(solution)/shard_map/project/pallas_call | solution.py:198
  41.6 0.1 collective-permute-start.6
  41.8 2.0 %collective-permute-start.9 = (bf16[64,2048]{1,0:T(8,128)(2,1)S(1)}, bf16[64,2048]{1,0:T(8,128)(2,1)S(1)}, u32[]{:S(2)}, u32[]{:S(2)}) collective-permute-start(bf16[64,2048]{1,0:T(8,128)(2,1)S(1)} %get-tuple-element.50), channel_id=1, source_target_pairs={{0,2},{1,3},{2,0},{3,1},{4,6},{5,7},{6,4},{7,5},{8,10},{9,11},{10,... | collective-permute-start | bytes 786440 | tf_op jit(solution)/shard_map/gather_input_block2_first64/ppermute | solution.py:54
  43.8 5.6 %backward_heads.1 = (bf16[512,512]{1,0:T(8,128)(2,1)S(1)}, bf16[512,512]{1,0:T(8,128)(2,1)S(1)}, bf16[512,512]{1,0:T(8,128)(2,1)S(1)}) custom-call(bf16[128,2048]{1,0:T(8,128)(2,1)S(1)} %cast.1.refs_2_.refs_0_, bf16[128,2048]{1,0:T(8,128)(2,1)S(1)} %collective-permute-done.1.refs_3_.refs_1_, bf16[128,2048]{1,0:T(8,128)(2,1)S(1)} %collective-permute-done.refs_2_, ...), custom_call_target="tpu_custom_call" | custom-call | flops 8000000000 | bytes 1 | tf_op jit(solution)/shard_map/backward_heads/pallas_call | solution.py:198
  49.4 1.6 %collective-permute-start.12 = (bf16[64,2048]{1,0:T(8,128)(2,1)S(1)}, bf16[64,2048]{1,0:T(8,128)(2,1)S(1)}, u32[]{:S(2)}, u32[]{:S(2)}) collective-permute-start(bf16[64,2048]{1,0:T(8,128)(2,1)S(1)} %get-tuple-element.56.refs_6_), channel_id=1, source_target_pairs={{0,1},{1,0},{2,3},{3,2},{4,5},{5,4},{6,7},{7,6},{8,9},{9,8},{10,11... | collective-permute-start | bytes 786440 | tf_op jit(solution)/shard_map/gather_input_block3_row0/ppermute | solution.py:54
  51.0 0.5 collective-permute-start.13
  51.5 3.4 %backward_terms.1 = (f32[128,2048]{1,0:T(8,128)S(1)}, bf16[128,2048]{1,0:T(8,128)(2,1)S(1)}, bf16[128,2048]{1,0:T(8,128)(2,1)S(1)}, f32[64,2048]{1,0:T(8,128)S(1)}, f32[64,2048]{1,0:T(8,128)S(1)}) custom-call(bf16[512,512]{1,0:T(8,128)(2,1)S(1)} %get-tuple-element.55.refs_2_.refs_0_, bf16[512,512]{1,0:T(8,128)(2,1)S(1)} %get-tuple-element.66.refs_1_, ...), custom_call_target="tpu_custom_call" | custom-call | flops 3000000000 | bytes 1 | tf_op jit(solution)/shard_map/backward_terms/pallas_call | solution.py:198
  54.9 1.4 %collective-permute-start.17 = (bf16[128,2048]{1,0:T(8,128)(2,1)S(1)}, bf16[128,2048]{1,0:T(8,128)(2,1)S(1)}, u32[]{:S(2)}, u32[]{:S(2)}) collective-permute-start(bf16[128,2048]{1,0:T(8,128)(2,1)S(1)} %get-tuple-element.70), channel_id=1, source_target_pairs={{0,1},{1,0},{2,3},{3,2},{4,5},{5,4},{6,7},{7,6},{8,9},{9,8},{10,11... | collective-permute-start | bytes 1572872 | tf_op jit(solution)/shard_map/scatter_grad_block3_part0/ppermute | solution.py:54
  56.3 0.7 collective-permute-start.18
  57.0 1.7 %collective-permute-done.12.refs_6_ = bf16[64,2048]{1,0:T(8,128)(2,1)S(1)} collective-permute-done((bf16[64,2048]{1,0:T(8,128)(2,1)S(1)}, bf16[64,2048]{1,0:T(8,128)(2,1)S(1)}, u32[]{:S(2)}, u32[]{:S(2)}) %collective-permute-start.12) | collective-permute-done | bytes 262176 | tf_op jit(solution)/shard_map/gather_input_block3_row0/ppermute | solution.py:54
  58.7 1.7 %collective-permute-done.13.refs_7_ = bf16[64,2048]{1,0:T(8,128)(2,1)S(1)} collective-permute-done((bf16[64,2048]{1,0:T(8,128)(2,1)S(1)}, bf16[64,2048]{1,0:T(8,128)(2,1)S(1)}, u32[]{:S(2)}, u32[]{:S(2)}) %collective-permute-start.13) | collective-permute-done | bytes 262176 | tf_op jit(solution)/shard_map/gather_input_block3_row64/ppermute | solution.py:54
  60.4 3.8 %project.3 = (bf16[512,512]{1,0:T(8,128)(2,1)S(1)}, bf16[512,512]{1,0:T(8,128)(2,1)S(1)}, bf16[512,512]{1,0:T(8,128)(2,1)S(1)}) custom-call(bf16[64,2048]{1,0:T(8,128)(2,1)S(1)} %get-tuple-element.46.refs_0_, bf16[64,2048]{1,0:T(8,128)(2,1)S(1)} %get-tuple-element.47.refs_1_, bf16[64,2048]{1,0:T(8,128)(2,1)S(1)} %collective-permute-done.6.refs_2_, ...), custom_call_target="tpu_custom_call" | custom-call | flops 5000000000 | bytes 1 | tf_op jit(solution)/shard_map/project/pallas_call | solution.py:198
  64.2 2.8 %forward_terms.1 = (bf16[128,2048]{1,0:T(8,128)(2,1)S(1)}, bf16[64,2048]{1,0:T(8,128)(2,1)S(1)}, bf16[64,2048]{1,0:T(8,128)(2,1)S(1)}, f32[128,2048]{1,0:T(8,128)S(1)}, f32[128,2048]{1,0:T(8,128)S(1)}) custom-call(bf16[512,512]{1,0:T(8,128)(2,1)S(1)} %get-tuple-element.58.refs_0_, bf16[512,512]{1,0:T(8,128)(2,1)S(1)} %get-tuple-element.59.refs_1_, ...), custom_call_target="tpu_custom_call" | custom-call | flops 5000000000 | bytes 1 | tf_op jit(solution)/shard_map/forward_terms/pallas_call | solution.py:198
  67.0 1.6 %collective-permute-start.16 = (bf16[64,2048]{1,0:T(8,128)(2,1)S(1)}, bf16[64,2048]{1,0:T(8,128)(2,1)S(1)}, u32[]{:S(2)}, u32[]{:S(2)}) collective-permute-start(bf16[64,2048]{1,0:T(8,128)(2,1)S(1)} %get-tuple-element.65), channel_id=1, source_target_pairs={{0,2},{1,3},{2,0},{3,1},{4,6},{5,7},{6,4},{7,5},{8,10},{9,11},{10,... | collective-permute-start | bytes 786440 | tf_op jit(solution)/shard_map/scatter_branch_block3_part1/ppermute | solution.py:54
  68.6 0.5 collective-permute-start.15
  69.2 2.4 %collective-permute-done.18.refs_3_ = bf16[128,2048]{1,0:T(8,128)(2,1)S(1)} collective-permute-done((bf16[128,2048]{1,0:T(8,128)(2,1)S(1)}, bf16[128,2048]{1,0:T(8,128)(2,1)S(1)}, u32[]{:S(2)}, u32[]{:S(2)}) %collective-permute-start.18) | collective-permute-done | bytes 524320 | tf_op jit(solution)/shard_map/scatter_grad_block3_part1/ppermute | solution.py:54
  71.6 0.1 sum_rows.2
  71.7 1.6 %collective-permute-start.22 = (bf16[64,2048]{1,0:T(8,128)(2,1)S(1)}, bf16[64,2048]{1,0:T(8,128)(2,1)S(1)}, u32[]{:S(2)}, u32[]{:S(2)}) collective-permute-start(bf16[64,2048]{1,0:T(8,128)(2,1)S(1)} %get-tuple-element.72.refs_4_), channel_id=1, source_target_pairs={{0,2},{1,3},{2,0},{3,1},{4,6},{5,7},{6,4},{7,5},{8,10},{9,11},{10,... | collective-permute-start | bytes 786440 | tf_op jit(solution)/shard_map/scatter_grad_block2_part0/ppermute | solution.py:54
  73.3 0.5 collective-permute-start.21
  73.8 3.4 %collective-permute-done.16.refs_3_ = bf16[64,2048]{1,0:T(8,128)(2,1)S(1)} collective-permute-done((bf16[64,2048]{1,0:T(8,128)(2,1)S(1)}, bf16[64,2048]{1,0:T(8,128)(2,1)S(1)}, u32[]{:S(2)}, u32[]{:S(2)}) %collective-permute-start.16) | collective-permute-done | bytes 262176 | tf_op jit(solution)/shard_map/scatter_branch_block3_part1/ppermute | solution.py:54
  77.2 0.2 sum_rows.3
  77.5 2.8 %collective-permute-start.20 = (bf16[128,2048]{1,0:T(8,128)(2,1)S(1)}, bf16[128,2048]{1,0:T(8,128)(2,1)S(1)}, u32[]{:S(2)}, u32[]{:S(2)}) collective-permute-start(bf16[128,2048]{1,0:T(8,128)(2,1)S(1)} %get-tuple-element.75.refs_6_), channel_id=1, source_target_pairs={{0,5},{1,4},{2,7},{3,6},{4,9},{5,8},{6,11},{7,10},{8,13},{9,12},{1... | collective-permute-start | bytes 1572872 | tf_op jit(solution)/shard_map/scatter_branch_block1_part0/ppermute | solution.py:64
  80.3 1.1 %collective-permute-done.22.refs_2_ = bf16[64,2048]{1,0:T(8,128)(2,1)S(1)} collective-permute-done((bf16[64,2048]{1,0:T(8,128)(2,1)S(1)}, bf16[64,2048]{1,0:T(8,128)(2,1)S(1)}, u32[]{:S(2)}, u32[]{:S(2)}) %collective-permute-start.22) | collective-permute-done | bytes 262176 | tf_op jit(solution)/shard_map/scatter_grad_block2_part0/ppermute | solution.py:54
  81.4 0.5 input_grad.1
  82.0 1.9 %collective-permute-start.23 = (bf16[128,2048]{1,0:T(8,128)(2,1)S(1)}, bf16[128,2048]{1,0:T(8,128)(2,1)S(1)}, u32[]{:S(2)}, u32[]{:S(2)}) collective-permute-start(bf16[128,2048]{1,0:T(8,128)(2,1)S(1)} %input_grad.1), channel_id=1, source_target_pairs={{0,28},{4,0},{8,4},{12,8},{16,12},{20,16},{24,20},{28,24},{1,29},{... | collective-permute-start | bytes 1572872 | tf_op jit(solution)/shard_map/ppermute | solution.py:70
  83.9 7.8 %collective-permute-done.19.refs_0_.refs_1_ = bf16[128,2048]{1,0:T(8,128)(2,1)S(1)} collective-permute-done((bf16[128,2048]{1,0:T(8,128)(2,1)S(1)}, bf16[128,2048]{1,0:T(8,128)(2,1)S(1)}, u32[]{:S(2)}, u32[]{:S(2)}) %collective-permute-start.19) | collective-permute-done | bytes 524320 | tf_op jit(solution)/shard_map/scatter_branch_block2_part0/ppermute | solution.py:64
  91.7 8.5 %collective-permute-done.20.refs_2_.refs_3_ = bf16[128,2048]{1,0:T(8,128)(2,1)S(1)} collective-permute-done((bf16[128,2048]{1,0:T(8,128)(2,1)S(1)}, bf16[128,2048]{1,0:T(8,128)(2,1)S(1)}, u32[]{:S(2)}, u32[]{:S(2)}) %collective-permute-start.20) | collective-permute-done | bytes 524320 | tf_op jit(solution)/shard_map/scatter_branch_block1_part0/ppermute | solution.py:64
  100.2 1.1 %activation_sum.1 = (f32[1,128,2048]{2,1,0:T(8,128)}, f32[8,128]{1,0:T(8,128)S(1)}) custom-call(bf16[128,2048]{1,0:T(8,128)(2,1)S(1)} %collective-permute-done.14.base_ref.refs_4_, bf16[128,2048]{1,0:T(8,128)(2,1)S(1)} %collective-permute-done.19.refs_0_.refs_1_, bf16[128,2048]{1,0:T(8,128)(2,1)S(1)} %collective-permute-done.19.refs_0_.refs_1_, ...), custom_call_target="tpu_custom_call" | custom-call | flops 8000000000 | bytes 1 | tf_op jit(solution)/shard_map/activation_sum/pallas_call | solution.py:198
  101.3 1.1 %widen.1 = f32[1,128,2048]{2,1,0:T(8,128)} custom-call(bf16[128,2048]{1,0:T(8,128)(2,1)S(1)} %collective-permute-done.23.in_any, f32[8,128]{1,0:T(8,128)S(1)} %get-tuple-element.79.refs_0_), custom_call_target="tpu_custom_call" | custom-call | flops 1 | bytes 1 | tf_op jit(solution)/shard_map/widen/pallas_call | solution.py:198
  (42 shorter events, 0.6 us)
Async XLA Ops:
  0.6 8.2 %copy-start.5 = (f32[1,128,2048]{2,1,0:T(8,128)S(1)}, f32[1,128,2048]{2,1,0:T(8,128)}, u32[]{:S(2)}) copy-start(f32[1,128,2048]{2,1,0:T(8,128)} %param.10) | copy-start | bytes 3145732
  3.0 5.8 %copy-start.3 = (bf16[128,2048]{1,0:T(8,128)(2,1)S(1)}, bf16[128,2048]{1,0:T(8,128)(2,1)}, u32[]{:S(2)}) copy-start(bf16[128,2048]{1,0:T(8,128)(2,1)} %get-tuple-element.43.refs_0_) | copy-start | bytes 1572868
  3.0 16.0 %collective-permute-start.3 = (bf16[128,2048]{1,0:T(8,128)(2,1)}, bf16[128,2048]{1,0:T(8,128)(2,1)S(1)}, u32[]{:S(2)}, u32[]{:S(2)}) collective-permute-start(bf16[128,2048]{1,0:T(8,128)(2,1)} %get-tuple-element.43.refs_0_), channel_id=1, source_target_pairs={{0,1},{1,0},{2,3},{3,2},{4,5},{5,4},{6,7},{7,6},{8,9},{9,8},{10,11... | collective-permute-start | bytes 1572872 | tf_op jit(solution)/shard_map/gather_saved_block1/ppermute | solution.py:54
  6.0 15.1 %collective-permute-start.2 = (bf16[128,2048]{1,0:T(8,128)(2,1)}, bf16[128,2048]{1,0:T(8,128)(2,1)S(1)}, u32[]{:S(2)}, u32[]{:S(2)}) collective-permute-start(bf16[128,2048]{1,0:T(8,128)(2,1)} %get-tuple-element.43.refs_0_), channel_id=1, source_target_pairs={{0,2},{1,3},{2,0},{3,1},{4,6},{5,7},{6,4},{7,5},{8,10},{9,11},{10,... | collective-permute-start | bytes 1572872 | tf_op jit(solution)/shard_map/gather_saved_block2/ppermute | solution.py:54
  8.8 14.4 %copy-start.4 = (f32[1,128,2048]{2,1,0:T(8,128)S(1)}, f32[1,128,2048]{2,1,0:T(8,128)}, u32[]{:S(2)}) copy-start(f32[1,128,2048]{2,1,0:T(8,128)} %param.8) | copy-start | bytes 3145732
  8.9 14.4 %copy-start.7 = (f32[1,2048]{1,0:T(1,128)S(1)}, f32[1,2048]{1,0:T(1,128)}, u32[]{:S(2)}) copy-start(f32[1,2048]{1,0:T(1,128)} %gain_ref.1) | copy-start | bytes 24580
  8.9 29.1 %copy-start.2 = (bf16[1,2048,512]{2,1,0:T(8,128)(2,1)S(1)}, bf16[1,2048,512]{2,1,0:T(8,128)(2,1)}, u32[]{:S(2)}) copy-start(bf16[1,2048,512]{2,1,0:T(8,128)(2,1)} %param.14) | copy-start | bytes 6291460
  8.9 29.0 %copy-start = (bf16[1,2048,512]{2,1,0:T(8,128)(2,1)S(1)}, bf16[1,2048,512]{2,1,0:T(8,128)(2,1)}, u32[]{:S(2)}) copy-start(bf16[1,2048,512]{2,1,0:T(8,128)(2,1)} %param.12) | copy-start | bytes 6291460
  9.0 29.0 %copy-start.1 = (bf16[1,2048,512]{2,1,0:T(8,128)(2,1)S(1)}, bf16[1,2048,512]{2,1,0:T(8,128)(2,1)}, u32[]{:S(2)}) copy-start(bf16[1,2048,512]{2,1,0:T(8,128)(2,1)} %param.13) | copy-start | bytes 6291460
  9.0 21.2 %collective-permute-start.1 = (bf16[128,2048]{1,0:T(8,128)(2,1)S(1)}, bf16[128,2048]{1,0:T(8,128)(2,1)S(1)}, u32[]{:S(2)}, u32[]{:S(2)}) collective-permute-start(bf16[128,2048]{1,0:T(8,128)(2,1)S(1)} %cast.1.refs_2_.refs_0_), channel_id=1, source_target_pairs={{0,1},{1,0},{2,3},{3,2},{4,5},{5,4},{6,7},{7,6},{8,9},{9,8},{10,11... | collective-permute-start | bytes 1572872 | tf_op jit(solution)/shard_map/gather_grad_block1/ppermute | solution.py:54
  9.6 22.7 %collective-permute-start = (bf16[128,2048]{1,0:T(8,128)(2,1)S(1)}, bf16[128,2048]{1,0:T(8,128)(2,1)S(1)}, u32[]{:S(2)}, u32[]{:S(2)}) collective-permute-start(bf16[128,2048]{1,0:T(8,128)(2,1)S(1)} %cast.1.refs_2_.refs_0_), channel_id=1, source_target_pairs={{0,2},{1,3},{2,0},{3,1},{4,6},{5,7},{6,4},{7,5},{8,10},{9,11},{10,... | collective-permute-start | bytes 1572872 | tf_op jit(solution)/shard_map/gather_grad_block2/ppermute | solution.py:54
  21.1 14.7 %collective-permute-start.4 = (bf16[64,2048]{1,0:T(8,128)(2,1)S(1)}, bf16[64,2048]{1,0:T(8,128)(2,1)S(1)}, u32[]{:S(2)}, u32[]{:S(2)}) collective-permute-start(bf16[64,2048]{1,0:T(8,128)(2,1)S(1)} %get-tuple-element.44.refs_4_), channel_id=1, source_target_pairs={{0,1},{1,0},{2,3},{3,2},{4,5},{5,4},{6,7},{7,6},{8,9},{9,8},{10,11... | collective-permute-start | bytes 786440 | tf_op jit(solution)/shard_map/gather_saved_block3_row0/ppermute | solution.py:54
  21.3 16.7 %collective-permute-start.5 = (bf16[64,2048]{1,0:T(8,128)(2,1)S(1)}, bf16[64,2048]{1,0:T(8,128)(2,1)S(1)}, u32[]{:S(2)}, u32[]{:S(2)}) collective-permute-start(bf16[64,2048]{1,0:T(8,128)(2,1)S(1)} %get-tuple-element.45.refs_5_), channel_id=1, source_target_pairs={{0,2},{1,3},{2,0},{3,1},{4,6},{5,7},{6,4},{7,5},{8,10},{9,11},{10,... | collective-permute-start | bytes 786440 | tf_op jit(solution)/shard_map/gather_saved_block3_row64/ppermute | solution.py:54
  32.4 9.3 %collective-permute-start.10 = (bf16[64,2048]{1,0:T(8,128)(2,1)S(1)}, bf16[64,2048]{1,0:T(8,128)(2,1)S(1)}, u32[]{:S(2)}, u32[]{:S(2)}) collective-permute-start(bf16[64,2048]{1,0:T(8,128)(2,1)S(1)} %get-tuple-element.51), channel_id=1, source_target_pairs={{0,1},{1,0},{2,3},{3,2},{4,5},{5,4},{6,7},{7,6},{8,9},{9,8},{10,11... | collective-permute-start | bytes 786440 | tf_op jit(solution)/shard_map/gather_grad_block3_row0/ppermute | solution.py:54
  32.5 11.2 %collective-permute-start.11 = (bf16[64,2048]{1,0:T(8,128)(2,1)S(1)}, bf16[64,2048]{1,0:T(8,128)(2,1)S(1)}, u32[]{:S(2)}, u32[]{:S(2)}) collective-permute-start(bf16[64,2048]{1,0:T(8,128)(2,1)S(1)} %get-tuple-element.52), channel_id=1, source_target_pairs={{0,2},{1,3},{2,0},{3,1},{4,6},{5,7},{6,4},{7,5},{8,10},{9,11},{10,... | collective-permute-start | bytes 786440 | tf_op jit(solution)/shard_map/gather_grad_block3_row64/ppermute | solution.py:54
  34.5 14.8 %collective-permute-start.8 = (bf16[64,2048]{1,0:T(8,128)(2,1)S(1)}, bf16[64,2048]{1,0:T(8,128)(2,1)S(1)}, u32[]{:S(2)}, u32[]{:S(2)}) collective-permute-start(bf16[64,2048]{1,0:T(8,128)(2,1)S(1)} %get-tuple-element.46.refs_0_), channel_id=1, source_target_pairs={{0,2},{1,3},{2,0},{3,1},{4,6},{5,7},{6,4},{7,5},{8,10},{9,11},{10,... | collective-permute-start | bytes 786440 | tf_op jit(solution)/shard_map/gather_input_block2_first0/ppermute | solution.py:54
  35.8 13.5 %collective-permute-start.7 = (bf16[64,2048]{1,0:T(8,128)(2,1)S(1)}, bf16[64,2048]{1,0:T(8,128)(2,1)S(1)}, u32[]{:S(2)}, u32[]{:S(2)}) collective-permute-start(bf16[64,2048]{1,0:T(8,128)(2,1)S(1)} %get-tuple-element.47.refs_1_), channel_id=1, source_target_pairs={{0,1},{1,0},{2,3},{3,2},{4,5},{5,4},{6,7},{7,6},{8,9},{9,8},{10,11... | collective-permute-start | bytes 786440 | tf_op jit(solution)/shard_map/gather_input_block1_first64/ppermute | solution.py:54
  37.9 5.8 %copy-start.8 = (bf16[1,2048,512]{2,1,0:T(8,128)(2,1)S(1)}, bf16[1,2048,512]{2,1,0:T(8,128)(2,1)}, u32[]{:S(2)}) copy-start(bf16[1,2048,512]{2,1,0:T(8,128)(2,1)} %param.15) | copy-start | bytes 6291460
  41.6 14.7 %collective-permute-start.6 = (bf16[64,2048]{1,0:T(8,128)(2,1)S(1)}, bf16[64,2048]{1,0:T(8,128)(2,1)S(1)}, u32[]{:S(2)}, u32[]{:S(2)}) collective-permute-start(bf16[64,2048]{1,0:T(8,128)(2,1)S(1)} %get-tuple-element.49), channel_id=1, source_target_pairs={{0,1},{1,0},{2,3},{3,2},{4,5},{5,4},{6,7},{7,6},{8,9},{9,8},{10,11... | collective-permute-start | bytes 786440 | tf_op jit(solution)/shard_map/gather_input_block1_first0/ppermute | solution.py:54
  41.8 15.3 %collective-permute-start.9 = (bf16[64,2048]{1,0:T(8,128)(2,1)S(1)}, bf16[64,2048]{1,0:T(8,128)(2,1)S(1)}, u32[]{:S(2)}, u32[]{:S(2)}) collective-permute-start(bf16[64,2048]{1,0:T(8,128)(2,1)S(1)} %get-tuple-element.50), channel_id=1, source_target_pairs={{0,2},{1,3},{2,0},{3,1},{4,6},{5,7},{6,4},{7,5},{8,10},{9,11},{10,... | collective-permute-start | bytes 786440 | tf_op jit(solution)/shard_map/gather_input_block2_first64/ppermute | solution.py:54
  49.4 9.3 %collective-permute-start.12 = (bf16[64,2048]{1,0:T(8,128)(2,1)S(1)}, bf16[64,2048]{1,0:T(8,128)(2,1)S(1)}, u32[]{:S(2)}, u32[]{:S(2)}) collective-permute-start(bf16[64,2048]{1,0:T(8,128)(2,1)S(1)} %get-tuple-element.56.refs_6_), channel_id=1, source_target_pairs={{0,1},{1,0},{2,3},{3,2},{4,5},{5,4},{6,7},{7,6},{8,9},{9,8},{10,11... | collective-permute-start | bytes 786440 | tf_op jit(solution)/shard_map/gather_input_block3_row0/ppermute | solution.py:54
  51.0 9.4 %collective-permute-start.13 = (bf16[64,2048]{1,0:T(8,128)(2,1)S(1)}, bf16[64,2048]{1,0:T(8,128)(2,1)S(1)}, u32[]{:S(2)}, u32[]{:S(2)}) collective-permute-start(bf16[64,2048]{1,0:T(8,128)(2,1)S(1)} %get-tuple-element.57.refs_7_), channel_id=1, source_target_pairs={{0,2},{1,3},{2,0},{3,1},{4,6},{5,7},{6,4},{7,5},{8,10},{9,11},{10,... | collective-permute-start | bytes 786440 | tf_op jit(solution)/shard_map/gather_input_block3_row64/ppermute | solution.py:54
  54.9 14.3 %collective-permute-start.17 = (bf16[128,2048]{1,0:T(8,128)(2,1)S(1)}, bf16[128,2048]{1,0:T(8,128)(2,1)S(1)}, u32[]{:S(2)}, u32[]{:S(2)}) collective-permute-start(bf16[128,2048]{1,0:T(8,128)(2,1)S(1)} %get-tuple-element.70), channel_id=1, source_target_pairs={{0,1},{1,0},{2,3},{3,2},{4,5},{5,4},{6,7},{7,6},{8,9},{9,8},{10,11... | collective-permute-start | bytes 1572872 | tf_op jit(solution)/shard_map/scatter_grad_block3_part0/ppermute | solution.py:54
  56.3 15.3 %collective-permute-start.18 = (bf16[128,2048]{1,0:T(8,128)(2,1)S(1)}, bf16[128,2048]{1,0:T(8,128)(2,1)S(1)}, u32[]{:S(2)}, u32[]{:S(2)}) collective-permute-start(bf16[128,2048]{1,0:T(8,128)(2,1)S(1)} %get-tuple-element.71), channel_id=1, source_target_pairs={{0,2},{1,3},{2,0},{3,1},{4,6},{5,7},{6,4},{7,5},{8,10},{9,11},{10,... | collective-permute-start | bytes 1572872 | tf_op jit(solution)/shard_map/scatter_grad_block3_part1/ppermute | solution.py:54
  67.0 10.2 %collective-permute-start.16 = (bf16[64,2048]{1,0:T(8,128)(2,1)S(1)}, bf16[64,2048]{1,0:T(8,128)(2,1)S(1)}, u32[]{:S(2)}, u32[]{:S(2)}) collective-permute-start(bf16[64,2048]{1,0:T(8,128)(2,1)S(1)} %get-tuple-element.65), channel_id=1, source_target_pairs={{0,2},{1,3},{2,0},{3,1},{4,6},{5,7},{6,4},{7,5},{8,10},{9,11},{10,... | collective-permute-start | bytes 786440 | tf_op jit(solution)/shard_map/scatter_branch_block3_part1/ppermute | solution.py:54
  68.6 8.6 %collective-permute-start.15 = (bf16[64,2048]{1,0:T(8,128)(2,1)S(1)}, bf16[64,2048]{1,0:T(8,128)(2,1)S(1)}, u32[]{:S(2)}, u32[]{:S(2)}) collective-permute-start(bf16[64,2048]{1,0:T(8,128)(2,1)S(1)} %get-tuple-element.64.refs_4_), channel_id=1, source_target_pairs={{0,1},{1,0},{2,3},{3,2},{4,5},{5,4},{6,7},{7,6},{8,9},{9,8},{10,11... | collective-permute-start | bytes 786440 | tf_op jit(solution)/shard_map/scatter_branch_block3_part0/ppermute | solution.py:54
  69.2 11.1 %collective-permute-start.14 = (bf16[128,2048]{1,0:T(8,128)(2,1)S(1)}, bf16[128,2048]{1,0:T(8,128)(2,1)S(1)}, u32[]{:S(2)}, u32[]{:S(2)}) collective-permute-start(bf16[128,2048]{1,0:T(8,128)(2,1)S(1)} %get-tuple-element.61), channel_id=1, source_target_pairs={{0,4},{1,5},{2,6},{3,7},{4,8},{5,9},{6,10},{7,11},{8,12},{9,13},{1... | collective-permute-start | bytes 1572872 | tf_op jit(solution)/shard_map/ppermute | solution.py:64
  71.7 9.7 %collective-permute-start.22 = (bf16[64,2048]{1,0:T(8,128)(2,1)S(1)}, bf16[64,2048]{1,0:T(8,128)(2,1)S(1)}, u32[]{:S(2)}, u32[]{:S(2)}) collective-permute-start(bf16[64,2048]{1,0:T(8,128)(2,1)S(1)} %get-tuple-element.72.refs_4_), channel_id=1, source_target_pairs={{0,2},{1,3},{2,0},{3,1},{4,6},{5,7},{6,4},{7,5},{8,10},{9,11},{10,... | collective-permute-start | bytes 786440 | tf_op jit(solution)/shard_map/scatter_grad_block2_part0/ppermute | solution.py:54
  73.3 8.1 %collective-permute-start.21 = (bf16[64,2048]{1,0:T(8,128)(2,1)S(1)}, bf16[64,2048]{1,0:T(8,128)(2,1)S(1)}, u32[]{:S(2)}, u32[]{:S(2)}) collective-permute-start(bf16[64,2048]{1,0:T(8,128)(2,1)S(1)} %get-tuple-element.73.refs_5_), channel_id=1, source_target_pairs={{0,1},{1,0},{2,3},{3,2},{4,5},{5,4},{6,7},{7,6},{8,9},{9,8},{10,11... | collective-permute-start | bytes 786440 | tf_op jit(solution)/shard_map/scatter_grad_block1_part1/ppermute | solution.py:54
  77.2 4.2 %copy-start.6 = (f32[1,128,2048]{2,1,0:T(8,128)S(1)}, f32[1,128,2048]{2,1,0:T(8,128)}, u32[]{:S(2)}) copy-start(f32[1,128,2048]{2,1,0:T(8,128)} %param.9) | copy-start | bytes 3145732
  77.2 4.2 %copy-start.9 = (f32[128,1]{1,0:T(8,128)S(1)}, f32[128,1]{1,0:T(8,128)}, u32[]{:S(2)}) copy-start(f32[128,1]{1,0:T(8,128)} %get-tuple-element.78.inv_ref) | copy-start | bytes 1540
  77.4 14.2 %collective-permute-start.19 = (bf16[128,2048]{1,0:T(8,128)(2,1)S(1)}, bf16[128,2048]{1,0:T(8,128)(2,1)S(1)}, u32[]{:S(2)}, u32[]{:S(2)}) collective-permute-start(bf16[128,2048]{1,0:T(8,128)(2,1)S(1)} %get-tuple-element.74.refs_5_), channel_id=1, source_target_pairs={{0,6},{1,7},{2,4},{3,5},{4,10},{5,11},{6,8},{7,9},{8,14},{9,15},{1... | collective-permute-start | bytes 1572872 | tf_op jit(solution)/shard_map/scatter_branch_block2_part0/ppermute | solution.py:64
  77.5 22.7 %collective-permute-start.20 = (bf16[128,2048]{1,0:T(8,128)(2,1)S(1)}, bf16[128,2048]{1,0:T(8,128)(2,1)S(1)}, u32[]{:S(2)}, u32[]{:S(2)}) collective-permute-start(bf16[128,2048]{1,0:T(8,128)(2,1)S(1)} %get-tuple-element.75.refs_6_), channel_id=1, source_target_pairs={{0,5},{1,4},{2,7},{3,6},{4,9},{5,8},{6,11},{7,10},{8,13},{9,12},{1... | collective-permute-start | bytes 1572872 | tf_op jit(solution)/shard_map/scatter_branch_block1_part0/ppermute | solution.py:64
  82.0 19.4 %collective-permute-start.23 = (bf16[128,2048]{1,0:T(8,128)(2,1)S(1)}, bf16[128,2048]{1,0:T(8,128)(2,1)S(1)}, u32[]{:S(2)}, u32[]{:S(2)}) collective-permute-start(bf16[128,2048]{1,0:T(8,128)(2,1)S(1)} %input_grad.1), channel_id=1, source_target_pairs={{0,28},{4,0},{8,4},{12,8},{16,12},{20,16},{24,20},{28,24},{1,29},{... | collective-permute-start | bytes 1572872 | tf_op jit(solution)/shard_map/ppermute | solution.py:70

commit v2 on v1

--- a/solution.py
+++ b/solution.py
@@ -19,7 +19,7 @@
 INPUT_GRAD_WEIGHT = 8_000_000_000
 LAST_SUM_WEIGHT = 8_000_000_000
 FORWARD_WEIGHT = 5_000_000_000
-SUMS_WEIGHT = 6000000000
+SUMS_WEIGHT = 1_000_000_000
 MIB = 1024 * 1024
 
 

time: 103 us -> 100 us (0.971)
  the two profiles are of different devices: /device:TPU:0 before, /device:TPU:1 now
where the time goes in v2:
time: 100 us
  waiting for transfers between devices  49 us (49%)
  Pallas kernels  25.8 us (26%)
  starting transfers between devices  22.8 us (23%)
  other arithmetic  1.29 us (1%)
  between operations  1.07 us (1%)
    ppermute x20, waiting for transfers between devices, across(): return lax.ppermute(value, 'seq', [(i, i ^ 1 << bit) for i in range(count)])  35.4 us
    pallas_call x17, Pallas kernels, call(): pl.pallas_call(kernel, out_shape=out_shapes, in_specs=in_specs, out_specs...  25.8 us
    ppermute x20, starting transfers between devices, across(): return lax.ppermute(value, 'seq', [(i, i ^ 1 << bit) for i in range(count)])  16.4 us
    ppermute x3, waiting for transfers between devices, across_and_on(): return lax.ppermute(value, ('pipe', 'seq'), pairs)  11.3 us
    ppermute x3, starting transfers between devices, across_and_on(): return lax.ppermute(value, ('pipe', 'seq'), pairs)  6.39 us
    ppermute x1, waiting for transfers between devices, passed_along(): return lax.ppermute(value, axis, pairs)  2.26 us
  transfers between devices with their start and end apart: 24, of which 15 were waited for; matrix products, arithmetic and copies ran while one was open for 1% of the time, Pallas kernels for 22%

profile of v2, /device:TPU:1, one launch (start us, length us, event | category | flops | bytes accessed | tf_op | source)
XLA Modules:
  0.0 100.0 jit_solution(2501611442997065118)
XLA Ops:
  0.6 2.3 %norm.3 = (bf16[128,2048]{1,0:T(8,128)(2,1)}, f32[128,1]{1,0:T(8,128)}) custom-call(f32[128,2048]{1,0:T(8,128)} %bitcast.22, f32[1,2048]{1,0:T(1,128)} %gain_ref.1), custom_call_target="tpu_custom_call" | custom-call | flops 1 | bytes 1 | tf_op jit(solution)/shard_map/norm/pallas_call | solution.py:198
  3.0 2.1 %collective-permute-start.3 = (bf16[128,2048]{1,0:T(8,128)(2,1)}, bf16[128,2048]{1,0:T(8,128)(2,1)S(1)}, u32[]{:S(2)}, u32[]{:S(2)}) collective-permute-start(bf16[128,2048]{1,0:T(8,128)(2,1)} %get-tuple-element.43.refs_0_), channel_id=1, source_target_pairs={{0,1},{1,0},{2,3},{3,2},{4,5},{5,4},{6,7},{7,6},{8,9},{9,8},{10,11... | collective-permute-start | bytes 1572872 | tf_op jit(solution)/shard_map/gather_saved_block1/ppermute | solution.py:54
  5.1 1.2 %collective-permute-start.2 = (bf16[128,2048]{1,0:T(8,128)(2,1)}, bf16[128,2048]{1,0:T(8,128)(2,1)S(1)}, u32[]{:S(2)}, u32[]{:S(2)}) collective-permute-start(bf16[128,2048]{1,0:T(8,128)(2,1)} %get-tuple-element.43.refs_0_), channel_id=1, source_target_pairs={{0,2},{1,3},{2,0},{3,1},{4,6},{5,7},{6,4},{7,5},{8,10},{9,11},{10,... | collective-permute-start | bytes 1572872 | tf_op jit(solution)/shard_map/gather_saved_block2/ppermute | solution.py:54
  6.4 1.0 fusion
  7.4 0.2 pad_maximum_fusion
  7.8 0.3 collective-permute-start.1
  8.2 8.8 %collective-permute-done.3.refs_1_ = bf16[128,2048]{1,0:T(8,128)(2,1)S(1)} collective-permute-done((bf16[128,2048]{1,0:T(8,128)(2,1)}, bf16[128,2048]{1,0:T(8,128)(2,1)S(1)}, u32[]{:S(2)}, u32[]{:S(2)}) %collective-permute-start.3) | collective-permute-done | bytes 524320 | tf_op jit(solution)/shard_map/gather_saved_block1/ppermute | solution.py:54
  17.0 0.8 collective-permute-done.2.refs_0_.refs_2_
  17.9 0.5 collective-permute-start.4
  18.3 1.1 %collective-permute-start.5 = (bf16[64,2048]{1,0:T(8,128)(2,1)S(1)}, bf16[64,2048]{1,0:T(8,128)(2,1)S(1)}, u32[]{:S(2)}, u32[]{:S(2)}) collective-permute-start(bf16[64,2048]{1,0:T(8,128)(2,1)S(1)} %get-tuple-element.45.refs_5_), channel_id=1, source_target_pairs={{0,2},{1,3},{2,0},{3,1},{4,6},{5,7},{6,4},{7,5},{8,10},{9,11},{10,... | collective-permute-start | bytes 786440 | tf_op jit(solution)/shard_map/gather_saved_block3_row64/ppermute | solution.py:54
  19.5 0.9 norm.2
  20.4 7.8 %collective-permute-done.1.refs_3_.refs_1_ = bf16[128,2048]{1,0:T(8,128)(2,1)S(1)} collective-permute-done((bf16[128,2048]{1,0:T(8,128)(2,1)S(1)}, bf16[128,2048]{1,0:T(8,128)(2,1)S(1)}, u32[]{:S(2)}, u32[]{:S(2)}) %collective-permute-start.1) | collective-permute-done | bytes 524320 | tf_op jit(solution)/shard_map/gather_grad_block1/ppermute | solution.py:54
  28.2 0.8 collective-permute-done.refs_2_
  29.1 0.5 collective-permute-start.10
  29.6 1.1 %collective-permute-start.11 = (bf16[64,2048]{1,0:T(8,128)(2,1)S(1)}, bf16[64,2048]{1,0:T(8,128)(2,1)S(1)}, u32[]{:S(2)}, u32[]{:S(2)}) collective-permute-start(bf16[64,2048]{1,0:T(8,128)(2,1)S(1)} %get-tuple-element.52), channel_id=1, source_target_pairs={{0,2},{1,3},{2,0},{3,1},{4,6},{5,7},{6,4},{7,5},{8,10},{9,11},{10,... | collective-permute-start | bytes 786440 | tf_op jit(solution)/shard_map/gather_grad_block3_row64/ppermute | solution.py:54
  30.8 0.3 collective-permute-start.8
  31.1 2.7 %collective-permute-done.4.refs_3_ = bf16[64,2048]{1,0:T(8,128)(2,1)S(1)} collective-permute-done((bf16[64,2048]{1,0:T(8,128)(2,1)S(1)}, bf16[64,2048]{1,0:T(8,128)(2,1)S(1)}, u32[]{:S(2)}, u32[]{:S(2)}) %collective-permute-start.4) | collective-permute-done | bytes 262176 | tf_op jit(solution)/shard_map/gather_saved_block3_row0/ppermute | solution.py:54
  33.8 1.1 %collective-permute-start.7 = (bf16[64,2048]{1,0:T(8,128)(2,1)S(1)}, bf16[64,2048]{1,0:T(8,128)(2,1)S(1)}, u32[]{:S(2)}, u32[]{:S(2)}) collective-permute-start(bf16[64,2048]{1,0:T(8,128)(2,1)S(1)} %get-tuple-element.47.refs_1_), channel_id=1, source_target_pairs={{0,1},{1,0},{2,3},{3,2},{4,5},{5,4},{6,7},{7,6},{8,9},{9,8},{10,11... | collective-permute-start | bytes 786440 | tf_op jit(solution)/shard_map/gather_input_block1_first64/ppermute | solution.py:54
  35.0 3.6 %project.2 = (bf16[512,512]{1,0:T(8,128)(2,1)S(1)}, bf16[512,512]{1,0:T(8,128)(2,1)S(1)}, bf16[512,512]{1,0:T(8,128)(2,1)S(1)}) custom-call(bf16[128,2048]{1,0:T(8,128)(2,1)S(1)} %copy-done.3, bf16[128,2048]{1,0:T(8,128)(2,1)S(1)} %collective-permute-done.3.refs_1_, bf16[128,2048]{1,0:T(8,128)(2,1)S(1)} %collective-permute-done.2.refs_0_.refs_2_, ...), custom_call_target="tpu_custom_call" | custom-call | flops 1 | bytes 1 | tf_op jit(solution)/shard_map/project/pallas_call | solution.py:198
  38.7 0.4 collective-permute-start.6
  39.1 1.5 %collective-permute-start.9 = (bf16[64,2048]{1,0:T(8,128)(2,1)S(1)}, bf16[64,2048]{1,0:T(8,128)(2,1)S(1)}, u32[]{:S(2)}, u32[]{:S(2)}) collective-permute-start(bf16[64,2048]{1,0:T(8,128)(2,1)S(1)} %get-tuple-element.50), channel_id=1, source_target_pairs={{0,2},{1,3},{2,0},{3,1},{4,6},{5,7},{6,4},{7,5},{8,10},{9,11},{10,... | collective-permute-start | bytes 786440 | tf_op jit(solution)/shard_map/gather_input_block2_first64/ppermute | solution.py:54
  40.6 5.6 %backward_heads.1 = (bf16[512,512]{1,0:T(8,128)(2,1)S(1)}, bf16[512,512]{1,0:T(8,128)(2,1)S(1)}, bf16[512,512]{1,0:T(8,128)(2,1)S(1)}) custom-call(bf16[128,2048]{1,0:T(8,128)(2,1)S(1)} %cast.1.refs_2_.refs_0_, bf16[128,2048]{1,0:T(8,128)(2,1)S(1)} %collective-permute-done.1.refs_3_.refs_1_, bf16[128,2048]{1,0:T(8,128)(2,1)S(1)} %collective-permute-done.refs_2_, ...), custom_call_target="tpu_custom_call" | custom-call | flops 8000000000 | bytes 1 | tf_op jit(solution)/shard_map/backward_heads/pallas_call | solution.py:198
  46.3 1.3 %collective-permute-start.12 = (bf16[64,2048]{1,0:T(8,128)(2,1)S(1)}, bf16[64,2048]{1,0:T(8,128)(2,1)S(1)}, u32[]{:S(2)}, u32[]{:S(2)}) collective-permute-start(bf16[64,2048]{1,0:T(8,128)(2,1)S(1)} %get-tuple-element.56.refs_6_), channel_id=1, source_target_pairs={{0,1},{1,0},{2,3},{3,2},{4,5},{5,4},{6,7},{7,6},{8,9},{9,8},{10,11... | collective-permute-start | bytes 786440 | tf_op jit(solution)/shard_map/gather_input_block3_row0/ppermute | solution.py:54
  47.5 0.2 collective-permute-start.13
  47.8 3.4 %backward_terms.1 = (f32[128,2048]{1,0:T(8,128)S(1)}, bf16[128,2048]{1,0:T(8,128)(2,1)S(1)}, bf16[128,2048]{1,0:T(8,128)(2,1)S(1)}, f32[64,2048]{1,0:T(8,128)S(1)}, f32[64,2048]{1,0:T(8,128)S(1)}) custom-call(bf16[512,512]{1,0:T(8,128)(2,1)S(1)} %get-tuple-element.55.refs_2_.refs_0_, bf16[512,512]{1,0:T(8,128)(2,1)S(1)} %get-tuple-element.66.refs_1_, ...), custom_call_target="tpu_custom_call" | custom-call | flops 3000000000 | bytes 1 | tf_op jit(solution)/shard_map/backward_terms/pallas_call | solution.py:198
  51.2 1.0 %collective-permute-start.17 = (bf16[128,2048]{1,0:T(8,128)(2,1)S(1)}, bf16[128,2048]{1,0:T(8,128)(2,1)S(1)}, u32[]{:S(2)}, u32[]{:S(2)}) collective-permute-start(bf16[128,2048]{1,0:T(8,128)(2,1)S(1)} %get-tuple-element.70), channel_id=1, source_target_pairs={{0,1},{1,0},{2,3},{3,2},{4,5},{5,4},{6,7},{7,6},{8,9},{9,8},{10,11... | collective-permute-start | bytes 1572872 | tf_op jit(solution)/shard_map/scatter_grad_block3_part0/ppermute | solution.py:54
  52.2 0.5 collective-permute-start.18
  52.8 3.1 %collective-permute-done.12.refs_6_ = bf16[64,2048]{1,0:T(8,128)(2,1)S(1)} collective-permute-done((bf16[64,2048]{1,0:T(8,128)(2,1)S(1)}, bf16[64,2048]{1,0:T(8,128)(2,1)S(1)}, u32[]{:S(2)}, u32[]{:S(2)}) %collective-permute-start.12) | collective-permute-done | bytes 262176 | tf_op jit(solution)/shard_map/gather_input_block3_row0/ppermute | solution.py:54
  55.9 1.3 %collective-permute-done.13.refs_7_ = bf16[64,2048]{1,0:T(8,128)(2,1)S(1)} collective-permute-done((bf16[64,2048]{1,0:T(8,128)(2,1)S(1)}, bf16[64,2048]{1,0:T(8,128)(2,1)S(1)}, u32[]{:S(2)}, u32[]{:S(2)}) %collective-permute-start.13) | collective-permute-done | bytes 262176 | tf_op jit(solution)/shard_map/gather_input_block3_row64/ppermute | solution.py:54
  57.1 3.8 %project.3 = (bf16[512,512]{1,0:T(8,128)(2,1)S(1)}, bf16[512,512]{1,0:T(8,128)(2,1)S(1)}, bf16[512,512]{1,0:T(8,128)(2,1)S(1)}) custom-call(bf16[64,2048]{1,0:T(8,128)(2,1)S(1)} %get-tuple-element.46.refs_0_, bf16[64,2048]{1,0:T(8,128)(2,1)S(1)} %get-tuple-element.47.refs_1_, bf16[64,2048]{1,0:T(8,128)(2,1)S(1)} %collective-permute-done.6.refs_2_, ...), custom_call_target="tpu_custom_call" | custom-call | flops 5000000000 | bytes 1 | tf_op jit(solution)/shard_map/project/pallas_call | solution.py:198
  60.9 2.8 %forward_terms.1 = (bf16[128,2048]{1,0:T(8,128)(2,1)S(1)}, bf16[64,2048]{1,0:T(8,128)(2,1)S(1)}, bf16[64,2048]{1,0:T(8,128)(2,1)S(1)}, f32[128,2048]{1,0:T(8,128)S(1)}, f32[128,2048]{1,0:T(8,128)S(1)}) custom-call(bf16[512,512]{1,0:T(8,128)(2,1)S(1)} %get-tuple-element.58.refs_0_, bf16[512,512]{1,0:T(8,128)(2,1)S(1)} %get-tuple-element.59.refs_1_, ...), custom_call_target="tpu_custom_call" | custom-call | flops 5000000000 | bytes 1 | tf_op jit(solution)/shard_map/forward_terms/pallas_call | solution.py:198
  63.8 4.6 %collective-permute-start.14 = (bf16[128,2048]{1,0:T(8,128)(2,1)S(1)}, bf16[128,2048]{1,0:T(8,128)(2,1)S(1)}, u32[]{:S(2)}, u32[]{:S(2)}) collective-permute-start(bf16[128,2048]{1,0:T(8,128)(2,1)S(1)} %get-tuple-element.61), channel_id=1, source_target_pairs={{0,4},{1,5},{2,6},{3,7},{4,8},{5,9},{6,10},{7,11},{8,12},{9,13},{1... | collective-permute-start | bytes 1572872 | tf_op jit(solution)/shard_map/ppermute | solution.py:64
  68.3 1.2 %collective-permute-start.16 = (bf16[64,2048]{1,0:T(8,128)(2,1)S(1)}, bf16[64,2048]{1,0:T(8,128)(2,1)S(1)}, u32[]{:S(2)}, u32[]{:S(2)}) collective-permute-start(bf16[64,2048]{1,0:T(8,128)(2,1)S(1)} %get-tuple-element.65), channel_id=1, source_target_pairs={{0,2},{1,3},{2,0},{3,1},{4,6},{5,7},{6,4},{7,5},{8,10},{9,11},{10,... | collective-permute-start | bytes 786440 | tf_op jit(solution)/shard_map/scatter_branch_block3_part1/ppermute | solution.py:54
  69.6 0.3 collective-permute-start.15
  69.9 0.3 collective-permute-start.22
  70.2 1.2 %collective-permute-start.21 = (bf16[64,2048]{1,0:T(8,128)(2,1)S(1)}, bf16[64,2048]{1,0:T(8,128)(2,1)S(1)}, u32[]{:S(2)}, u32[]{:S(2)}) collective-permute-start(bf16[64,2048]{1,0:T(8,128)(2,1)S(1)} %get-tuple-element.73.refs_5_), channel_id=1, source_target_pairs={{0,1},{1,0},{2,3},{3,2},{4,5},{5,4},{6,7},{7,6},{8,9},{9,8},{10,11... | collective-permute-start | bytes 786440 | tf_op jit(solution)/shard_map/scatter_grad_block1_part1/ppermute | solution.py:54
  71.4 5.1 %collective-permute-done.16.refs_3_ = bf16[64,2048]{1,0:T(8,128)(2,1)S(1)} collective-permute-done((bf16[64,2048]{1,0:T(8,128)(2,1)S(1)}, bf16[64,2048]{1,0:T(8,128)(2,1)S(1)}, u32[]{:S(2)}, u32[]{:S(2)}) %collective-permute-start.16) | collective-permute-done | bytes 262176 | tf_op jit(solution)/shard_map/scatter_branch_block3_part1/ppermute | solution.py:54
  76.6 1.2 %collective-permute-done.15.refs_2_ = bf16[64,2048]{1,0:T(8,128)(2,1)S(1)} collective-permute-done((bf16[64,2048]{1,0:T(8,128)(2,1)S(1)}, bf16[64,2048]{1,0:T(8,128)(2,1)S(1)}, u32[]{:S(2)}, u32[]{:S(2)}) %collective-permute-start.15) | collective-permute-done | bytes 262176 | tf_op jit(solution)/shard_map/scatter_branch_block3_part0/ppermute | solution.py:54
  77.9 1.0 %collective-permute-start.19 = (bf16[128,2048]{1,0:T(8,128)(2,1)S(1)}, bf16[128,2048]{1,0:T(8,128)(2,1)S(1)}, u32[]{:S(2)}, u32[]{:S(2)}) collective-permute-start(bf16[128,2048]{1,0:T(8,128)(2,1)S(1)} %get-tuple-element.74.refs_5_), channel_id=1, source_target_pairs={{0,6},{1,7},{2,4},{3,5},{4,10},{5,11},{6,8},{7,9},{8,14},{9,15},{1... | collective-permute-start | bytes 1572872 | tf_op jit(solution)/shard_map/scatter_branch_block2_part0/ppermute | solution.py:64
  79.0 0.8 collective-permute-start.20
  79.8 2.1 %collective-permute-done.22.refs_2_ = bf16[64,2048]{1,0:T(8,128)(2,1)S(1)} collective-permute-done((bf16[64,2048]{1,0:T(8,128)(2,1)S(1)}, bf16[64,2048]{1,0:T(8,128)(2,1)S(1)}, u32[]{:S(2)}, u32[]{:S(2)}) %collective-permute-start.22) | collective-permute-done | bytes 262176 | tf_op jit(solution)/shard_map/scatter_grad_block2_part0/ppermute | solution.py:54
  81.9 1.5 %collective-permute-done.21.refs_1_ = bf16[64,2048]{1,0:T(8,128)(2,1)S(1)} collective-permute-done((bf16[64,2048]{1,0:T(8,128)(2,1)S(1)}, bf16[64,2048]{1,0:T(8,128)(2,1)S(1)}, u32[]{:S(2)}, u32[]{:S(2)}) %collective-permute-start.21) | collective-permute-done | bytes 262176 | tf_op jit(solution)/shard_map/scatter_grad_block1_part1/ppermute | solution.py:54
  83.4 0.5 input_grad.1
  84.0 8.8 %collective-permute-done.19.refs_0_.refs_1_ = bf16[128,2048]{1,0:T(8,128)(2,1)S(1)} collective-permute-done((bf16[128,2048]{1,0:T(8,128)(2,1)S(1)}, bf16[128,2048]{1,0:T(8,128)(2,1)S(1)}, u32[]{:S(2)}, u32[]{:S(2)}) %collective-permute-start.19) | collective-permute-done | bytes 524320 | tf_op jit(solution)/shard_map/scatter_branch_block2_part0/ppermute | solution.py:64
  92.9 2.5 %collective-permute-done.20.refs_2_.refs_3_ = bf16[128,2048]{1,0:T(8,128)(2,1)S(1)} collective-permute-done((bf16[128,2048]{1,0:T(8,128)(2,1)S(1)}, bf16[128,2048]{1,0:T(8,128)(2,1)S(1)}, u32[]{:S(2)}, u32[]{:S(2)}) %collective-permute-start.20) | collective-permute-done | bytes 524320 | tf_op jit(solution)/shard_map/scatter_branch_block1_part0/ppermute | solution.py:64
  95.4 1.1 %activation_sum.1 = (f32[1,128,2048]{2,1,0:T(8,128)}, f32[8,128]{1,0:T(8,128)S(1)}) custom-call(bf16[128,2048]{1,0:T(8,128)(2,1)S(1)} %collective-permute-done.14.base_ref.refs_4_, bf16[128,2048]{1,0:T(8,128)(2,1)S(1)} %collective-permute-done.19.refs_0_.refs_1_, bf16[128,2048]{1,0:T(8,128)(2,1)S(1)} %collective-permute-done.19.refs_0_.refs_1_, ...), custom_call_target="tpu_custom_call" | custom-call | flops 8000000000 | bytes 1 | tf_op jit(solution)/shard_map/activation_sum/pallas_call | solution.py:198
  96.5 2.3 %collective-permute-done.23.in_any = bf16[128,2048]{1,0:T(8,128)(2,1)S(1)} collective-permute-done((bf16[128,2048]{1,0:T(8,128)(2,1)S(1)}, bf16[128,2048]{1,0:T(8,128)(2,1)S(1)}, u32[]{:S(2)}, u32[]{:S(2)}) %collective-permute-start.23) | collective-permute-done | bytes 524320 | tf_op jit(solution)/shard_map/ppermute | solution.py:70
  98.8 1.1 %widen.1 = f32[1,128,2048]{2,1,0:T(8,128)} custom-call(bf16[128,2048]{1,0:T(8,128)(2,1)S(1)} %collective-permute-done.23.in_any, f32[8,128]{1,0:T(8,128)S(1)} %get-tuple-element.79.refs_0_), custom_call_target="tpu_custom_call" | custom-call | flops 1 | bytes 1 | tf_op jit(solution)/shard_map/widen/pallas_call | solution.py:198
  (42 shorter events, 0.9 us)
Async XLA Ops:
  0.6 7.0 %copy-start.5 = (f32[1,128,2048]{2,1,0:T(8,128)S(1)}, f32[1,128,2048]{2,1,0:T(8,128)}, u32[]{:S(2)}) copy-start(f32[1,128,2048]{2,1,0:T(8,128)} %param.10) | copy-start | bytes 3145732
  3.0 4.7 %copy-start.3 = (bf16[128,2048]{1,0:T(8,128)(2,1)S(1)}, bf16[128,2048]{1,0:T(8,128)(2,1)}, u32[]{:S(2)}) copy-start(bf16[128,2048]{1,0:T(8,128)(2,1)} %get-tuple-element.43.refs_0_) | copy-start | bytes 1572868
  3.0 14.0 %collective-permute-start.3 = (bf16[128,2048]{1,0:T(8,128)(2,1)}, bf16[128,2048]{1,0:T(8,128)(2,1)S(1)}, u32[]{:S(2)}, u32[]{:S(2)}) collective-permute-start(bf16[128,2048]{1,0:T(8,128)(2,1)} %get-tuple-element.43.refs_0_), channel_id=1, source_target_pairs={{0,1},{1,0},{2,3},{3,2},{4,5},{5,4},{6,7},{7,6},{8,9},{9,8},{10,11... | collective-permute-start | bytes 1572872 | tf_op jit(solution)/shard_map/gather_saved_block1/ppermute | solution.py:54
  5.1 12.7 %collective-permute-start.2 = (bf16[128,2048]{1,0:T(8,128)(2,1)}, bf16[128,2048]{1,0:T(8,128)(2,1)S(1)}, u32[]{:S(2)}, u32[]{:S(2)}) collective-permute-start(bf16[128,2048]{1,0:T(8,128)(2,1)} %get-tuple-element.43.refs_0_), channel_id=1, source_target_pairs={{0,2},{1,3},{2,0},{3,1},{4,6},{5,7},{6,4},{7,5},{8,10},{9,11},{10,... | collective-permute-start | bytes 1572872 | tf_op jit(solution)/shard_map/gather_saved_block2/ppermute | solution.py:54
  7.7 11.8 %copy-start.4 = (f32[1,128,2048]{2,1,0:T(8,128)S(1)}, f32[1,128,2048]{2,1,0:T(8,128)}, u32[]{:S(2)}) copy-start(f32[1,128,2048]{2,1,0:T(8,128)} %param.8) | copy-start | bytes 3145732
  7.7 11.8 %copy-start.7 = (f32[1,2048]{1,0:T(1,128)S(1)}, f32[1,2048]{1,0:T(1,128)}, u32[]{:S(2)}) copy-start(f32[1,2048]{1,0:T(1,128)} %gain_ref.1) | copy-start | bytes 24580
  7.7 27.3 %copy-start.2 = (bf16[1,2048,512]{2,1,0:T(8,128)(2,1)S(1)}, bf16[1,2048,512]{2,1,0:T(8,128)(2,1)}, u32[]{:S(2)}) copy-start(bf16[1,2048,512]{2,1,0:T(8,128)(2,1)} %param.14) | copy-start | bytes 6291460
  7.8 27.2 %copy-start = (bf16[1,2048,512]{2,1,0:T(8,128)(2,1)S(1)}, bf16[1,2048,512]{2,1,0:T(8,128)(2,1)}, u32[]{:S(2)}) copy-start(bf16[1,2048,512]{2,1,0:T(8,128)(2,1)} %param.12) | copy-start | bytes 6291460
  7.8 27.2 %copy-start.1 = (bf16[1,2048,512]{2,1,0:T(8,128)(2,1)S(1)}, bf16[1,2048,512]{2,1,0:T(8,128)(2,1)}, u32[]{:S(2)}) copy-start(bf16[1,2048,512]{2,1,0:T(8,128)(2,1)} %param.13) | copy-start | bytes 6291460
  7.8 20.4 %collective-permute-start.1 = (bf16[128,2048]{1,0:T(8,128)(2,1)S(1)}, bf16[128,2048]{1,0:T(8,128)(2,1)S(1)}, u32[]{:S(2)}, u32[]{:S(2)}) collective-permute-start(bf16[128,2048]{1,0:T(8,128)(2,1)S(1)} %cast.1.refs_2_.refs_0_), channel_id=1, source_target_pairs={{0,1},{1,0},{2,3},{3,2},{4,5},{5,4},{6,7},{7,6},{8,9},{9,8},{10,11... | collective-permute-start | bytes 1572872 | tf_op jit(solution)/shard_map/gather_grad_block1/ppermute | solution.py:54
  8.1 20.9 %collective-permute-start = (bf16[128,2048]{1,0:T(8,128)(2,1)S(1)}, bf16[128,2048]{1,0:T(8,128)(2,1)S(1)}, u32[]{:S(2)}, u32[]{:S(2)}) collective-permute-start(bf16[128,2048]{1,0:T(8,128)(2,1)S(1)} %cast.1.refs_2_.refs_0_), channel_id=1, source_target_pairs={{0,2},{1,3},{2,0},{3,1},{4,6},{5,7},{6,4},{7,5},{8,10},{9,11},{10,... | collective-permute-start | bytes 1572872 | tf_op jit(solution)/shard_map/gather_grad_block2/ppermute | solution.py:54
  17.9 16.0 %collective-permute-start.4 = (bf16[64,2048]{1,0:T(8,128)(2,1)S(1)}, bf16[64,2048]{1,0:T(8,128)(2,1)S(1)}, u32[]{:S(2)}, u32[]{:S(2)}) collective-permute-start(bf16[64,2048]{1,0:T(8,128)(2,1)S(1)} %get-tuple-element.44.refs_4_), channel_id=1, source_target_pairs={{0,1},{1,0},{2,3},{3,2},{4,5},{5,4},{6,7},{7,6},{8,9},{9,8},{10,11... | collective-permute-start | bytes 786440 | tf_op jit(solution)/shard_map/gather_saved_block3_row0/ppermute | solution.py:54
  18.3 16.6 %collective-permute-start.5 = (bf16[64,2048]{1,0:T(8,128)(2,1)S(1)}, bf16[64,2048]{1,0:T(8,128)(2,1)S(1)}, u32[]{:S(2)}, u32[]{:S(2)}) collective-permute-start(bf16[64,2048]{1,0:T(8,128)(2,1)S(1)} %get-tuple-element.45.refs_5_), channel_id=1, source_target_pairs={{0,2},{1,3},{2,0},{3,1},{4,6},{5,7},{6,4},{7,5},{8,10},{9,11},{10,... | collective-permute-start | bytes 786440 | tf_op jit(solution)/shard_map/gather_saved_block3_row64/ppermute | solution.py:54
  29.1 10.0 %collective-permute-start.10 = (bf16[64,2048]{1,0:T(8,128)(2,1)S(1)}, bf16[64,2048]{1,0:T(8,128)(2,1)S(1)}, u32[]{:S(2)}, u32[]{:S(2)}) collective-permute-start(bf16[64,2048]{1,0:T(8,128)(2,1)S(1)} %get-tuple-element.51), channel_id=1, source_target_pairs={{0,1},{1,0},{2,3},{3,2},{4,5},{5,4},{6,7},{7,6},{8,9},{9,8},{10,11... | collective-permute-start | bytes 786440 | tf_op jit(solution)/shard_map/gather_grad_block3_row0/ppermute | solution.py:54
  29.6 11.0 %collective-permute-start.11 = (bf16[64,2048]{1,0:T(8,128)(2,1)S(1)}, bf16[64,2048]{1,0:T(8,128)(2,1)S(1)}, u32[]{:S(2)}, u32[]{:S(2)}) collective-permute-start(bf16[64,2048]{1,0:T(8,128)(2,1)S(1)} %get-tuple-element.52), channel_id=1, source_target_pairs={{0,2},{1,3},{2,0},{3,1},{4,6},{5,7},{6,4},{7,5},{8,10},{9,11},{10,... | collective-permute-start | bytes 786440 | tf_op jit(solution)/shard_map/gather_grad_block3_row64/ppermute | solution.py:54
  30.8 15.4 %collective-permute-start.8 = (bf16[64,2048]{1,0:T(8,128)(2,1)S(1)}, bf16[64,2048]{1,0:T(8,128)(2,1)S(1)}, u32[]{:S(2)}, u32[]{:S(2)}) collective-permute-start(bf16[64,2048]{1,0:T(8,128)(2,1)S(1)} %get-tuple-element.46.refs_0_), channel_id=1, source_target_pairs={{0,2},{1,3},{2,0},{3,1},{4,6},{5,7},{6,4},{7,5},{8,10},{9,11},{10,... | collective-permute-start | bytes 786440 | tf_op jit(solution)/shard_map/gather_input_block2_first0/ppermute | solution.py:54
  33.8 12.4 %collective-permute-start.7 = (bf16[64,2048]{1,0:T(8,128)(2,1)S(1)}, bf16[64,2048]{1,0:T(8,128)(2,1)S(1)}, u32[]{:S(2)}, u32[]{:S(2)}) collective-permute-start(bf16[64,2048]{1,0:T(8,128)(2,1)S(1)} %get-tuple-element.47.refs_1_), channel_id=1, source_target_pairs={{0,1},{1,0},{2,3},{3,2},{4,5},{5,4},{6,7},{7,6},{8,9},{9,8},{10,11... | collective-permute-start | bytes 786440 | tf_op jit(solution)/shard_map/gather_input_block1_first64/ppermute | solution.py:54
  35.0 5.6 %copy-start.8 = (bf16[1,2048,512]{2,1,0:T(8,128)(2,1)S(1)}, bf16[1,2048,512]{2,1,0:T(8,128)(2,1)}, u32[]{:S(2)}) copy-start(bf16[1,2048,512]{2,1,0:T(8,128)(2,1)} %param.15) | copy-start | bytes 6291460
  38.7 13.6 %collective-permute-start.6 = (bf16[64,2048]{1,0:T(8,128)(2,1)S(1)}, bf16[64,2048]{1,0:T(8,128)(2,1)S(1)}, u32[]{:S(2)}, u32[]{:S(2)}) collective-permute-start(bf16[64,2048]{1,0:T(8,128)(2,1)S(1)} %get-tuple-element.49), channel_id=1, source_target_pairs={{0,1},{1,0},{2,3},{3,2},{4,5},{5,4},{6,7},{7,6},{8,9},{9,8},{10,11... | collective-permute-start | bytes 786440 | tf_op jit(solution)/shard_map/gather_input_block1_first0/ppermute | solution.py:54
  39.1 13.6 %collective-permute-start.9 = (bf16[64,2048]{1,0:T(8,128)(2,1)S(1)}, bf16[64,2048]{1,0:T(8,128)(2,1)S(1)}, u32[]{:S(2)}, u32[]{:S(2)}) collective-permute-start(bf16[64,2048]{1,0:T(8,128)(2,1)S(1)} %get-tuple-element.50), channel_id=1, source_target_pairs={{0,2},{1,3},{2,0},{3,1},{4,6},{5,7},{6,4},{7,5},{8,10},{9,11},{10,... | collective-permute-start | bytes 786440 | tf_op jit(solution)/shard_map/gather_input_block2_first64/ppermute | solution.py:54
  46.3 9.6 %collective-permute-start.12 = (bf16[64,2048]{1,0:T(8,128)(2,1)S(1)}, bf16[64,2048]{1,0:T(8,128)(2,1)S(1)}, u32[]{:S(2)}, u32[]{:S(2)}) collective-permute-start(bf16[64,2048]{1,0:T(8,128)(2,1)S(1)} %get-tuple-element.56.refs_6_), channel_id=1, source_target_pairs={{0,1},{1,0},{2,3},{3,2},{4,5},{5,4},{6,7},{7,6},{8,9},{9,8},{10,11... | collective-permute-start | bytes 786440 | tf_op jit(solution)/shard_map/gather_input_block3_row0/ppermute | solution.py:54
  47.5 9.6 %collective-permute-start.13 = (bf16[64,2048]{1,0:T(8,128)(2,1)S(1)}, bf16[64,2048]{1,0:T(8,128)(2,1)S(1)}, u32[]{:S(2)}, u32[]{:S(2)}) collective-permute-start(bf16[64,2048]{1,0:T(8,128)(2,1)S(1)} %get-tuple-element.57.refs_7_), channel_id=1, source_target_pairs={{0,2},{1,3},{2,0},{3,1},{4,6},{5,7},{6,4},{7,5},{8,10},{9,11},{10,... | collective-permute-start | bytes 786440 | tf_op jit(solution)/shard_map/gather_input_block3_row64/ppermute | solution.py:54
  51.2 18.6 %collective-permute-start.17 = (bf16[128,2048]{1,0:T(8,128)(2,1)S(1)}, bf16[128,2048]{1,0:T(8,128)(2,1)S(1)}, u32[]{:S(2)}, u32[]{:S(2)}) collective-permute-start(bf16[128,2048]{1,0:T(8,128)(2,1)S(1)} %get-tuple-element.70), channel_id=1, source_target_pairs={{0,1},{1,0},{2,3},{3,2},{4,5},{5,4},{6,7},{7,6},{8,9},{9,8},{10,11... | collective-permute-start | bytes 1572872 | tf_op jit(solution)/shard_map/scatter_grad_block3_part0/ppermute | solution.py:54
  52.2 17.6 %collective-permute-start.18 = (bf16[128,2048]{1,0:T(8,128)(2,1)S(1)}, bf16[128,2048]{1,0:T(8,128)(2,1)S(1)}, u32[]{:S(2)}, u32[]{:S(2)}) collective-permute-start(bf16[128,2048]{1,0:T(8,128)(2,1)S(1)} %get-tuple-element.71), channel_id=1, source_target_pairs={{0,2},{1,3},{2,0},{3,1},{4,6},{5,7},{6,4},{7,5},{8,10},{9,11},{10,... | collective-permute-start | bytes 1572872 | tf_op jit(solution)/shard_map/scatter_grad_block3_part1/ppermute | solution.py:54
  63.8 16.0 %collective-permute-start.14 = (bf16[128,2048]{1,0:T(8,128)(2,1)S(1)}, bf16[128,2048]{1,0:T(8,128)(2,1)S(1)}, u32[]{:S(2)}, u32[]{:S(2)}) collective-permute-start(bf16[128,2048]{1,0:T(8,128)(2,1)S(1)} %get-tuple-element.61), channel_id=1, source_target_pairs={{0,4},{1,5},{2,6},{3,7},{4,8},{5,9},{6,10},{7,11},{8,12},{9,13},{1... | collective-permute-start | bytes 1572872 | tf_op jit(solution)/shard_map/ppermute | solution.py:64
  68.3 8.3 %collective-permute-start.16 = (bf16[64,2048]{1,0:T(8,128)(2,1)S(1)}, bf16[64,2048]{1,0:T(8,128)(2,1)S(1)}, u32[]{:S(2)}, u32[]{:S(2)}) collective-permute-start(bf16[64,2048]{1,0:T(8,128)(2,1)S(1)} %get-tuple-element.65), channel_id=1, source_target_pairs={{0,2},{1,3},{2,0},{3,1},{4,6},{5,7},{6,4},{7,5},{8,10},{9,11},{10,... | collective-permute-start | bytes 786440 | tf_op jit(solution)/shard_map/scatter_branch_block3_part1/ppermute | solution.py:54
  69.6 8.2 %collective-permute-start.15 = (bf16[64,2048]{1,0:T(8,128)(2,1)S(1)}, bf16[64,2048]{1,0:T(8,128)(2,1)S(1)}, u32[]{:S(2)}, u32[]{:S(2)}) collective-permute-start(bf16[64,2048]{1,0:T(8,128)(2,1)S(1)} %get-tuple-element.64.refs_4_), channel_id=1, source_target_pairs={{0,1},{1,0},{2,3},{3,2},{4,5},{5,4},{6,7},{7,6},{8,9},{9,8},{10,11... | collective-permute-start | bytes 786440 | tf_op jit(solution)/shard_map/scatter_branch_block3_part0/ppermute | solution.py:54
  69.9 13.5 %copy-start.6 = (f32[1,128,2048]{2,1,0:T(8,128)S(1)}, f32[1,128,2048]{2,1,0:T(8,128)}, u32[]{:S(2)}) copy-start(f32[1,128,2048]{2,1,0:T(8,128)} %param.9) | copy-start | bytes 3145732
  69.9 13.5 %copy-start.9 = (f32[128,1]{1,0:T(8,128)S(1)}, f32[128,1]{1,0:T(8,128)}, u32[]{:S(2)}) copy-start(f32[128,1]{1,0:T(8,128)} %get-tuple-element.78.inv_ref) | copy-start | bytes 1540
  69.9 12.0 %collective-permute-start.22 = (bf16[64,2048]{1,0:T(8,128)(2,1)S(1)}, bf16[64,2048]{1,0:T(8,128)(2,1)S(1)}, u32[]{:S(2)}, u32[]{:S(2)}) collective-permute-start(bf16[64,2048]{1,0:T(8,128)(2,1)S(1)} %get-tuple-element.72.refs_4_), channel_id=1, source_target_pairs={{0,2},{1,3},{2,0},{3,1},{4,6},{5,7},{6,4},{7,5},{8,10},{9,11},{10,... | collective-permute-start | bytes 786440 | tf_op jit(solution)/shard_map/scatter_grad_block2_part0/ppermute | solution.py:54
  70.2 13.2 %collective-permute-start.21 = (bf16[64,2048]{1,0:T(8,128)(2,1)S(1)}, bf16[64,2048]{1,0:T(8,128)(2,1)S(1)}, u32[]{:S(2)}, u32[]{:S(2)}) collective-permute-start(bf16[64,2048]{1,0:T(8,128)(2,1)S(1)} %get-tuple-element.73.refs_5_), channel_id=1, source_target_pairs={{0,1},{1,0},{2,3},{3,2},{4,5},{5,4},{6,7},{7,6},{8,9},{9,8},{10,11... | collective-permute-start | bytes 786440 | tf_op jit(solution)/shard_map/scatter_grad_block1_part1/ppermute | solution.py:54
  77.9 14.9 %collective-permute-start.19 = (bf16[128,2048]{1,0:T(8,128)(2,1)S(1)}, bf16[128,2048]{1,0:T(8,128)(2,1)S(1)}, u32[]{:S(2)}, u32[]{:S(2)}) collective-permute-start(bf16[128,2048]{1,0:T(8,128)(2,1)S(1)} %get-tuple-element.74.refs_5_), channel_id=1, source_target_pairs={{0,6},{1,7},{2,4},{3,5},{4,10},{5,11},{6,8},{7,9},{8,14},{9,15},{1... | collective-permute-start | bytes 1572872 | tf_op jit(solution)/shard_map/scatter_branch_block2_part0/ppermute | solution.py:64
  79.0 16.4 %collective-permute-start.20 = (bf16[128,2048]{1,0:T(8,128)(2,1)S(1)}, bf16[128,2048]{1,0:T(8,128)(2,1)S(1)}, u32[]{:S(2)}, u32[]{:S(2)}) collective-permute-start(bf16[128,2048]{1,0:T(8,128)(2,1)S(1)} %get-tuple-element.75.refs_6_), channel_id=1, source_target_pairs={{0,5},{1,4},{2,7},{3,6},{4,9},{5,8},{6,11},{7,10},{8,13},{9,12},{1... | collective-permute-start | bytes 1572872 | tf_op jit(solution)/shard_map/scatter_branch_block1_part0/ppermute | solution.py:64
  84.0 14.8 %collective-permute-start.23 = (bf16[128,2048]{1,0:T(8,128)(2,1)S(1)}, bf16[128,2048]{1,0:T(8,128)(2,1)S(1)}, u32[]{:S(2)}, u32[]{:S(2)}) collective-permute-start(bf16[128,2048]{1,0:T(8,128)(2,1)S(1)} %input_grad.1), channel_id=1, source_target_pairs={{0,28},{4,0},{8,4},{12,8},{16,12},{20,16},{24,20},{28,24},{1,29},{... | collective-permute-start | bytes 1572872 | tf_op jit(solution)/shard_map/ppermute | solution.py:70

commit v3 on v2

--- a/solution.py
+++ b/solution.py
@@ -10,7 +10,7 @@
 
 HD = 128
 LANES = 128
-CHUNK = 256
+CHUNK = 512
 EXP2_SCALE = HD ** (-0.5) * math.log2(math.e)
 NT = (((1,), (1,)), ((), ()))
 TN = (((0,), (0,)), ((), ()))

time: 100 us -> 100 us (level)
  no operation moved by 1% of the time
where the time goes in v3:
time: 100 us
  waiting for transfers between devices  49 us (49%)
  Pallas kernels  25.8 us (26%)
  starting transfers between devices  22.8 us (23%)
  other arithmetic  1.29 us (1%)
  between operations  1.07 us (1%)
    ppermute x20, waiting for transfers between devices, across(): return lax.ppermute(value, 'seq', [(i, i ^ 1 << bit) for i in range(count)])  35.4 us
    pallas_call x17, Pallas kernels, call(): pl.pallas_call(kernel, out_shape=out_shapes, in_specs=in_specs, out_specs...  25.8 us
    ppermute x20, starting transfers between devices, across(): return lax.ppermute(value, 'seq', [(i, i ^ 1 << bit) for i in range(count)])  16.4 us
    ppermute x3, waiting for transfers between devices, across_and_on(): return lax.ppermute(value, ('pipe', 'seq'), pairs)  11.3 us
    ppermute x3, starting transfers between devices, across_and_on(): return lax.ppermute(value, ('pipe', 'seq'), pairs)  6.39 us
    ppermute x1, waiting for transfers between devices, passed_along(): return lax.ppermute(value, axis, pairs)  2.26 us
  transfers between devices with their start and end apart: 24, of which 15 were waited for; matrix products, arithmetic and copies ran while one was open for 1% of the time, Pallas kernels for 22%

profile of v3, /device:TPU:1, one launch (start us, length us, event | category | flops | bytes accessed | tf_op | source)
XLA Modules:
  0.0 100.0 jit_solution(3188303152551726934)
XLA Ops:
  0.6 2.3 %norm.3 = (bf16[128,2048]{1,0:T(8,128)(2,1)}, f32[128,1]{1,0:T(8,128)}) custom-call(f32[128,2048]{1,0:T(8,128)} %bitcast.22, f32[1,2048]{1,0:T(1,128)} %gain_ref.1), custom_call_target="tpu_custom_call" | custom-call | flops 1 | bytes 1 | tf_op jit(solution)/shard_map/norm/pallas_call | solution.py:198
  3.0 2.1 %collective-permute-start.3 = (bf16[128,2048]{1,0:T(8,128)(2,1)}, bf16[128,2048]{1,0:T(8,128)(2,1)S(1)}, u32[]{:S(2)}, u32[]{:S(2)}) collective-permute-start(bf16[128,2048]{1,0:T(8,128)(2,1)} %get-tuple-element.43.refs_0_), channel_id=1, source_target_pairs={{0,1},{1,0},{2,3},{3,2},{4,5},{5,4},{6,7},{7,6},{8,9},{9,8},{10,11... | collective-permute-start | bytes 1572872 | tf_op jit(solution)/shard_map/gather_saved_block1/ppermute | solution.py:54
  5.1 1.2 %collective-permute-start.2 = (bf16[128,2048]{1,0:T(8,128)(2,1)}, bf16[128,2048]{1,0:T(8,128)(2,1)S(1)}, u32[]{:S(2)}, u32[]{:S(2)}) collective-permute-start(bf16[128,2048]{1,0:T(8,128)(2,1)} %get-tuple-element.43.refs_0_), channel_id=1, source_target_pairs={{0,2},{1,3},{2,0},{3,1},{4,6},{5,7},{6,4},{7,5},{8,10},{9,11},{10,... | collective-permute-start | bytes 1572872 | tf_op jit(solution)/shard_map/gather_saved_block2/ppermute | solution.py:54
  6.4 1.0 fusion
  7.4 0.2 pad_maximum_fusion
  7.8 0.3 collective-permute-start.1
  8.2 8.8 %collective-permute-done.3.refs_1_ = bf16[128,2048]{1,0:T(8,128)(2,1)S(1)} collective-permute-done((bf16[128,2048]{1,0:T(8,128)(2,1)}, bf16[128,2048]{1,0:T(8,128)(2,1)S(1)}, u32[]{:S(2)}, u32[]{:S(2)}) %collective-permute-start.3) | collective-permute-done | bytes 524320 | tf_op jit(solution)/shard_map/gather_saved_block1/ppermute | solution.py:54
  17.0 0.8 collective-permute-done.2.refs_0_.refs_2_
  17.9 0.5 collective-permute-start.4
  18.3 1.1 %collective-permute-start.5 = (bf16[64,2048]{1,0:T(8,128)(2,1)S(1)}, bf16[64,2048]{1,0:T(8,128)(2,1)S(1)}, u32[]{:S(2)}, u32[]{:S(2)}) collective-permute-start(bf16[64,2048]{1,0:T(8,128)(2,1)S(1)} %get-tuple-element.45.refs_5_), channel_id=1, source_target_pairs={{0,2},{1,3},{2,0},{3,1},{4,6},{5,7},{6,4},{7,5},{8,10},{9,11},{10,... | collective-permute-start | bytes 786440 | tf_op jit(solution)/shard_map/gather_saved_block3_row64/ppermute | solution.py:54
  19.5 0.9 norm.2
  20.4 7.8 %collective-permute-done.1.refs_3_.refs_1_ = bf16[128,2048]{1,0:T(8,128)(2,1)S(1)} collective-permute-done((bf16[128,2048]{1,0:T(8,128)(2,1)S(1)}, bf16[128,2048]{1,0:T(8,128)(2,1)S(1)}, u32[]{:S(2)}, u32[]{:S(2)}) %collective-permute-start.1) | collective-permute-done | bytes 524320 | tf_op jit(solution)/shard_map/gather_grad_block1/ppermute | solution.py:54
  28.2 0.8 collective-permute-done.refs_2_
  29.1 0.5 collective-permute-start.10
  29.6 1.1 %collective-permute-start.11 = (bf16[64,2048]{1,0:T(8,128)(2,1)S(1)}, bf16[64,2048]{1,0:T(8,128)(2,1)S(1)}, u32[]{:S(2)}, u32[]{:S(2)}) collective-permute-start(bf16[64,2048]{1,0:T(8,128)(2,1)S(1)} %get-tuple-element.52), channel_id=1, source_target_pairs={{0,2},{1,3},{2,0},{3,1},{4,6},{5,7},{6,4},{7,5},{8,10},{9,11},{10,... | collective-permute-start | bytes 786440 | tf_op jit(solution)/shard_map/gather_grad_block3_row64/ppermute | solution.py:54
  30.8 0.3 collective-permute-start.8
  31.1 2.7 %collective-permute-done.4.refs_3_ = bf16[64,2048]{1,0:T(8,128)(2,1)S(1)} collective-permute-done((bf16[64,2048]{1,0:T(8,128)(2,1)S(1)}, bf16[64,2048]{1,0:T(8,128)(2,1)S(1)}, u32[]{:S(2)}, u32[]{:S(2)}) %collective-permute-start.4) | collective-permute-done | bytes 262176 | tf_op jit(solution)/shard_map/gather_saved_block3_row0/ppermute | solution.py:54
  33.8 1.1 %collective-permute-start.7 = (bf16[64,2048]{1,0:T(8,128)(2,1)S(1)}, bf16[64,2048]{1,0:T(8,128)(2,1)S(1)}, u32[]{:S(2)}, u32[]{:S(2)}) collective-permute-start(bf16[64,2048]{1,0:T(8,128)(2,1)S(1)} %get-tuple-element.47.refs_1_), channel_id=1, source_target_pairs={{0,1},{1,0},{2,3},{3,2},{4,5},{5,4},{6,7},{7,6},{8,9},{9,8},{10,11... | collective-permute-start | bytes 786440 | tf_op jit(solution)/shard_map/gather_input_block1_first64/ppermute | solution.py:54
  35.0 3.6 %project.2 = (bf16[512,512]{1,0:T(8,128)(2,1)S(1)}, bf16[512,512]{1,0:T(8,128)(2,1)S(1)}, bf16[512,512]{1,0:T(8,128)(2,1)S(1)}) custom-call(bf16[128,2048]{1,0:T(8,128)(2,1)S(1)} %copy-done.3, bf16[128,2048]{1,0:T(8,128)(2,1)S(1)} %collective-permute-done.3.refs_1_, bf16[128,2048]{1,0:T(8,128)(2,1)S(1)} %collective-permute-done.2.refs_0_.refs_2_, ...), custom_call_target="tpu_custom_call" | custom-call | flops 1 | bytes 1 | tf_op jit(solution)/shard_map/project/pallas_call | solution.py:198
  38.7 0.4 collective-permute-start.6
  39.1 1.5 %collective-permute-start.9 = (bf16[64,2048]{1,0:T(8,128)(2,1)S(1)}, bf16[64,2048]{1,0:T(8,128)(2,1)S(1)}, u32[]{:S(2)}, u32[]{:S(2)}) collective-permute-start(bf16[64,2048]{1,0:T(8,128)(2,1)S(1)} %get-tuple-element.50), channel_id=1, source_target_pairs={{0,2},{1,3},{2,0},{3,1},{4,6},{5,7},{6,4},{7,5},{8,10},{9,11},{10,... | collective-permute-start | bytes 786440 | tf_op jit(solution)/shard_map/gather_input_block2_first64/ppermute | solution.py:54
  40.6 5.6 %backward_heads.1 = (bf16[512,512]{1,0:T(8,128)(2,1)S(1)}, bf16[512,512]{1,0:T(8,128)(2,1)S(1)}, bf16[512,512]{1,0:T(8,128)(2,1)S(1)}) custom-call(bf16[128,2048]{1,0:T(8,128)(2,1)S(1)} %cast.1.refs_2_.refs_0_, bf16[128,2048]{1,0:T(8,128)(2,1)S(1)} %collective-permute-done.1.refs_3_.refs_1_, bf16[128,2048]{1,0:T(8,128)(2,1)S(1)} %collective-permute-done.refs_2_, ...), custom_call_target="tpu_custom_call" | custom-call | flops 8000000000 | bytes 1 | tf_op jit(solution)/shard_map/backward_heads/pallas_call | solution.py:198
  46.3 1.3 %collective-permute-start.12 = (bf16[64,2048]{1,0:T(8,128)(2,1)S(1)}, bf16[64,2048]{1,0:T(8,128)(2,1)S(1)}, u32[]{:S(2)}, u32[]{:S(2)}) collective-permute-start(bf16[64,2048]{1,0:T(8,128)(2,1)S(1)} %get-tuple-element.56.refs_6_), channel_id=1, source_target_pairs={{0,1},{1,0},{2,3},{3,2},{4,5},{5,4},{6,7},{7,6},{8,9},{9,8},{10,11... | collective-permute-start | bytes 786440 | tf_op jit(solution)/shard_map/gather_input_block3_row0/ppermute | solution.py:54
  47.5 0.2 collective-permute-start.13
  47.8 3.4 %backward_terms.1 = (f32[128,2048]{1,0:T(8,128)S(1)}, bf16[128,2048]{1,0:T(8,128)(2,1)S(1)}, bf16[128,2048]{1,0:T(8,128)(2,1)S(1)}, f32[64,2048]{1,0:T(8,128)S(1)}, f32[64,2048]{1,0:T(8,128)S(1)}) custom-call(bf16[512,512]{1,0:T(8,128)(2,1)S(1)} %get-tuple-element.55.refs_2_.refs_0_, bf16[512,512]{1,0:T(8,128)(2,1)S(1)} %get-tuple-element.66.refs_1_, ...), custom_call_target="tpu_custom_call" | custom-call | flops 3000000000 | bytes 1 | tf_op jit(solution)/shard_map/backward_terms/pallas_call | solution.py:198
  51.2 1.0 %collective-permute-start.17 = (bf16[128,2048]{1,0:T(8,128)(2,1)S(1)}, bf16[128,2048]{1,0:T(8,128)(2,1)S(1)}, u32[]{:S(2)}, u32[]{:S(2)}) collective-permute-start(bf16[128,2048]{1,0:T(8,128)(2,1)S(1)} %get-tuple-element.70), channel_id=1, source_target_pairs={{0,1},{1,0},{2,3},{3,2},{4,5},{5,4},{6,7},{7,6},{8,9},{9,8},{10,11... | collective-permute-start | bytes 1572872 | tf_op jit(solution)/shard_map/scatter_grad_block3_part0/ppermute | solution.py:54
  52.2 0.5 collective-permute-start.18
  52.8 3.1 %collective-permute-done.12.refs_6_ = bf16[64,2048]{1,0:T(8,128)(2,1)S(1)} collective-permute-done((bf16[64,2048]{1,0:T(8,128)(2,1)S(1)}, bf16[64,2048]{1,0:T(8,128)(2,1)S(1)}, u32[]{:S(2)}, u32[]{:S(2)}) %collective-permute-start.12) | collective-permute-done | bytes 262176 | tf_op jit(solution)/shard_map/gather_input_block3_row0/ppermute | solution.py:54
  55.9 1.3 %collective-permute-done.13.refs_7_ = bf16[64,2048]{1,0:T(8,128)(2,1)S(1)} collective-permute-done((bf16[64,2048]{1,0:T(8,128)(2,1)S(1)}, bf16[64,2048]{1,0:T(8,128)(2,1)S(1)}, u32[]{:S(2)}, u32[]{:S(2)}) %collective-permute-start.13) | collective-permute-done | bytes 262176 | tf_op jit(solution)/shard_map/gather_input_block3_row64/ppermute | solution.py:54
  57.1 3.8 %project.3 = (bf16[512,512]{1,0:T(8,128)(2,1)S(1)}, bf16[512,512]{1,0:T(8,128)(2,1)S(1)}, bf16[512,512]{1,0:T(8,128)(2,1)S(1)}) custom-call(bf16[64,2048]{1,0:T(8,128)(2,1)S(1)} %get-tuple-element.46.refs_0_, bf16[64,2048]{1,0:T(8,128)(2,1)S(1)} %get-tuple-element.47.refs_1_, bf16[64,2048]{1,0:T(8,128)(2,1)S(1)} %collective-permute-done.6.refs_2_, ...), custom_call_target="tpu_custom_call" | custom-call | flops 5000000000 | bytes 1 | tf_op jit(solution)/shard_map/project/pallas_call | solution.py:198
  60.9 2.8 %forward_terms.1 = (bf16[128,2048]{1,0:T(8,128)(2,1)S(1)}, bf16[64,2048]{1,0:T(8,128)(2,1)S(1)}, bf16[64,2048]{1,0:T(8,128)(2,1)S(1)}, f32[128,2048]{1,0:T(8,128)S(1)}, f32[128,2048]{1,0:T(8,128)S(1)}) custom-call(bf16[512,512]{1,0:T(8,128)(2,1)S(1)} %get-tuple-element.58.refs_0_, bf16[512,512]{1,0:T(8,128)(2,1)S(1)} %get-tuple-element.59.refs_1_, ...), custom_call_target="tpu_custom_call" | custom-call | flops 5000000000 | bytes 1 | tf_op jit(solution)/shard_map/forward_terms/pallas_call | solution.py:198
  63.8 4.6 %collective-permute-start.14 = (bf16[128,2048]{1,0:T(8,128)(2,1)S(1)}, bf16[128,2048]{1,0:T(8,128)(2,1)S(1)}, u32[]{:S(2)}, u32[]{:S(2)}) collective-permute-start(bf16[128,2048]{1,0:T(8,128)(2,1)S(1)} %get-tuple-element.61), channel_id=1, source_target_pairs={{0,4},{1,5},{2,6},{3,7},{4,8},{5,9},{6,10},{7,11},{8,12},{9,13},{1... | collective-permute-start | bytes 1572872 | tf_op jit(solution)/shard_map/ppermute | solution.py:64
  68.3 1.2 %collective-permute-start.16 = (bf16[64,2048]{1,0:T(8,128)(2,1)S(1)}, bf16[64,2048]{1,0:T(8,128)(2,1)S(1)}, u32[]{:S(2)}, u32[]{:S(2)}) collective-permute-start(bf16[64,2048]{1,0:T(8,128)(2,1)S(1)} %get-tuple-element.65), channel_id=1, source_target_pairs={{0,2},{1,3},{2,0},{3,1},{4,6},{5,7},{6,4},{7,5},{8,10},{9,11},{10,... | collective-permute-start | bytes 786440 | tf_op jit(solution)/shard_map/scatter_branch_block3_part1/ppermute | solution.py:54
  69.6 0.3 collective-permute-start.15
  69.9 0.3 collective-permute-start.22
  70.2 1.2 %collective-permute-start.21 = (bf16[64,2048]{1,0:T(8,128)(2,1)S(1)}, bf16[64,2048]{1,0:T(8,128)(2,1)S(1)}, u32[]{:S(2)}, u32[]{:S(2)}) collective-permute-start(bf16[64,2048]{1,0:T(8,128)(2,1)S(1)} %get-tuple-element.73.refs_5_), channel_id=1, source_target_pairs={{0,1},{1,0},{2,3},{3,2},{4,5},{5,4},{6,7},{7,6},{8,9},{9,8},{10,11... | collective-permute-start | bytes 786440 | tf_op jit(solution)/shard_map/scatter_grad_block1_part1/ppermute | solution.py:54
  71.4 5.1 %collective-permute-done.16.refs_3_ = bf16[64,2048]{1,0:T(8,128)(2,1)S(1)} collective-permute-done((bf16[64,2048]{1,0:T(8,128)(2,1)S(1)}, bf16[64,2048]{1,0:T(8,128)(2,1)S(1)}, u32[]{:S(2)}, u32[]{:S(2)}) %collective-permute-start.16) | collective-permute-done | bytes 262176 | tf_op jit(solution)/shard_map/scatter_branch_block3_part1/ppermute | solution.py:54
  76.6 1.2 %collective-permute-done.15.refs_2_ = bf16[64,2048]{1,0:T(8,128)(2,1)S(1)} collective-permute-done((bf16[64,2048]{1,0:T(8,128)(2,1)S(1)}, bf16[64,2048]{1,0:T(8,128)(2,1)S(1)}, u32[]{:S(2)}, u32[]{:S(2)}) %collective-permute-start.15) | collective-permute-done | bytes 262176 | tf_op jit(solution)/shard_map/scatter_branch_block3_part0/ppermute | solution.py:54
  77.9 1.0 %collective-permute-start.19 = (bf16[128,2048]{1,0:T(8,128)(2,1)S(1)}, bf16[128,2048]{1,0:T(8,128)(2,1)S(1)}, u32[]{:S(2)}, u32[]{:S(2)}) collective-permute-start(bf16[128,2048]{1,0:T(8,128)(2,1)S(1)} %get-tuple-element.74.refs_5_), channel_id=1, source_target_pairs={{0,6},{1,7},{2,4},{3,5},{4,10},{5,11},{6,8},{7,9},{8,14},{9,15},{1... | collective-permute-start | bytes 1572872 | tf_op jit(solution)/shard_map/scatter_branch_block2_part0/ppermute | solution.py:64
  79.0 0.8 collective-permute-start.20
  79.8 2.1 %collective-permute-done.22.refs_2_ = bf16[64,2048]{1,0:T(8,128)(2,1)S(1)} collective-permute-done((bf16[64,2048]{1,0:T(8,128)(2,1)S(1)}, bf16[64,2048]{1,0:T(8,128)(2,1)S(1)}, u32[]{:S(2)}, u32[]{:S(2)}) %collective-permute-start.22) | collective-permute-done | bytes 262176 | tf_op jit(solution)/shard_map/scatter_grad_block2_part0/ppermute | solution.py:54
  81.9 1.5 %collective-permute-done.21.refs_1_ = bf16[64,2048]{1,0:T(8,128)(2,1)S(1)} collective-permute-done((bf16[64,2048]{1,0:T(8,128)(2,1)S(1)}, bf16[64,2048]{1,0:T(8,128)(2,1)S(1)}, u32[]{:S(2)}, u32[]{:S(2)}) %collective-permute-start.21) | collective-permute-done | bytes 262176 | tf_op jit(solution)/shard_map/scatter_grad_block1_part1/ppermute | solution.py:54
  83.4 0.5 input_grad.1
  84.0 8.8 %collective-permute-done.19.refs_0_.refs_1_ = bf16[128,2048]{1,0:T(8,128)(2,1)S(1)} collective-permute-done((bf16[128,2048]{1,0:T(8,128)(2,1)S(1)}, bf16[128,2048]{1,0:T(8,128)(2,1)S(1)}, u32[]{:S(2)}, u32[]{:S(2)}) %collective-permute-start.19) | collective-permute-done | bytes 524320 | tf_op jit(solution)/shard_map/scatter_branch_block2_part0/ppermute | solution.py:64
  92.9 2.5 %collective-permute-done.20.refs_2_.refs_3_ = bf16[128,2048]{1,0:T(8,128)(2,1)S(1)} collective-permute-done((bf16[128,2048]{1,0:T(8,128)(2,1)S(1)}, bf16[128,2048]{1,0:T(8,128)(2,1)S(1)}, u32[]{:S(2)}, u32[]{:S(2)}) %collective-permute-start.20) | collective-permute-done | bytes 524320 | tf_op jit(solution)/shard_map/scatter_branch_block1_part0/ppermute | solution.py:64
  95.4 1.1 %activation_sum.1 = (f32[1,128,2048]{2,1,0:T(8,128)}, f32[8,128]{1,0:T(8,128)S(1)}) custom-call(bf16[128,2048]{1,0:T(8,128)(2,1)S(1)} %collective-permute-done.14.base_ref.refs_4_, bf16[128,2048]{1,0:T(8,128)(2,1)S(1)} %collective-permute-done.19.refs_0_.refs_1_, bf16[128,2048]{1,0:T(8,128)(2,1)S(1)} %collective-permute-done.19.refs_0_.refs_1_, ...), custom_call_target="tpu_custom_call" | custom-call | flops 8000000000 | bytes 1 | tf_op jit(solution)/shard_map/activation_sum/pallas_call | solution.py:198
  96.5 2.3 %collective-permute-done.23.in_any = bf16[128,2048]{1,0:T(8,128)(2,1)S(1)} collective-permute-done((bf16[128,2048]{1,0:T(8,128)(2,1)S(1)}, bf16[128,2048]{1,0:T(8,128)(2,1)S(1)}, u32[]{:S(2)}, u32[]{:S(2)}) %collective-permute-start.23) | collective-permute-done | bytes 524320 | tf_op jit(solution)/shard_map/ppermute | solution.py:70
  98.8 1.1 %widen.1 = f32[1,128,2048]{2,1,0:T(8,128)} custom-call(bf16[128,2048]{1,0:T(8,128)(2,1)S(1)} %collective-permute-done.23.in_any, f32[8,128]{1,0:T(8,128)S(1)} %get-tuple-element.79.refs_0_), custom_call_target="tpu_custom_call" | custom-call | flops 1 | bytes 1 | tf_op jit(solution)/shard_map/widen/pallas_call | solution.py:198
  (42 shorter events, 0.9 us)
Async XLA Ops:
  0.6 7.0 %copy-start.5 = (f32[1,128,2048]{2,1,0:T(8,128)S(1)}, f32[1,128,2048]{2,1,0:T(8,128)}, u32[]{:S(2)}) copy-start(f32[1,128,2048]{2,1,0:T(8,128)} %param.10) | copy-start | bytes 3145732
  3.0 4.7 %copy-start.3 = (bf16[128,2048]{1,0:T(8,128)(2,1)S(1)}, bf16[128,2048]{1,0:T(8,128)(2,1)}, u32[]{:S(2)}) copy-start(bf16[128,2048]{1,0:T(8,128)(2,1)} %get-tuple-element.43.refs_0_) | copy-start | bytes 1572868
  3.0 14.0 %collective-permute-start.3 = (bf16[128,2048]{1,0:T(8,128)(2,1)}, bf16[128,2048]{1,0:T(8,128)(2,1)S(1)}, u32[]{:S(2)}, u32[]{:S(2)}) collective-permute-start(bf16[128,2048]{1,0:T(8,128)(2,1)} %get-tuple-element.43.refs_0_), channel_id=1, source_target_pairs={{0,1},{1,0},{2,3},{3,2},{4,5},{5,4},{6,7},{7,6},{8,9},{9,8},{10,11... | collective-permute-start | bytes 1572872 | tf_op jit(solution)/shard_map/gather_saved_block1/ppermute | solution.py:54
  5.1 12.7 %collective-permute-start.2 = (bf16[128,2048]{1,0:T(8,128)(2,1)}, bf16[128,2048]{1,0:T(8,128)(2,1)S(1)}, u32[]{:S(2)}, u32[]{:S(2)}) collective-permute-start(bf16[128,2048]{1,0:T(8,128)(2,1)} %get-tuple-element.43.refs_0_), channel_id=1, source_target_pairs={{0,2},{1,3},{2,0},{3,1},{4,6},{5,7},{6,4},{7,5},{8,10},{9,11},{10,... | collective-permute-start | bytes 1572872 | tf_op jit(solution)/shard_map/gather_saved_block2/ppermute | solution.py:54
  7.7 11.8 %copy-start.4 = (f32[1,128,2048]{2,1,0:T(8,128)S(1)}, f32[1,128,2048]{2,1,0:T(8,128)}, u32[]{:S(2)}) copy-start(f32[1,128,2048]{2,1,0:T(8,128)} %param.8) | copy-start | bytes 3145732
  7.7 11.8 %copy-start.7 = (f32[1,2048]{1,0:T(1,128)S(1)}, f32[1,2048]{1,0:T(1,128)}, u32[]{:S(2)}) copy-start(f32[1,2048]{1,0:T(1,128)} %gain_ref.1) | copy-start | bytes 24580
  7.7 27.3 %copy-start.2 = (bf16[1,2048,512]{2,1,0:T(8,128)(2,1)S(1)}, bf16[1,2048,512]{2,1,0:T(8,128)(2,1)}, u32[]{:S(2)}) copy-start(bf16[1,2048,512]{2,1,0:T(8,128)(2,1)} %param.14) | copy-start | bytes 6291460
  7.8 27.2 %copy-start = (bf16[1,2048,512]{2,1,0:T(8,128)(2,1)S(1)}, bf16[1,2048,512]{2,1,0:T(8,128)(2,1)}, u32[]{:S(2)}) copy-start(bf16[1,2048,512]{2,1,0:T(8,128)(2,1)} %param.12) | copy-start | bytes 6291460
  7.8 27.2 %copy-start.1 = (bf16[1,2048,512]{2,1,0:T(8,128)(2,1)S(1)}, bf16[1,2048,512]{2,1,0:T(8,128)(2,1)}, u32[]{:S(2)}) copy-start(bf16[1,2048,512]{2,1,0:T(8,128)(2,1)} %param.13) | copy-start | bytes 6291460
  7.8 20.4 %collective-permute-start.1 = (bf16[128,2048]{1,0:T(8,128)(2,1)S(1)}, bf16[128,2048]{1,0:T(8,128)(2,1)S(1)}, u32[]{:S(2)}, u32[]{:S(2)}) collective-permute-start(bf16[128,2048]{1,0:T(8,128)(2,1)S(1)} %cast.1.refs_2_.refs_0_), channel_id=1, source_target_pairs={{0,1},{1,0},{2,3},{3,2},{4,5},{5,4},{6,7},{7,6},{8,9},{9,8},{10,11... | collective-permute-start | bytes 1572872 | tf_op jit(solution)/shard_map/gather_grad_block1/ppermute | solution.py:54
  8.1 20.9 %collective-permute-start = (bf16[128,2048]{1,0:T(8,128)(2,1)S(1)}, bf16[128,2048]{1,0:T(8,128)(2,1)S(1)}, u32[]{:S(2)}, u32[]{:S(2)}) collective-permute-start(bf16[128,2048]{1,0:T(8,128)(2,1)S(1)} %cast.1.refs_2_.refs_0_), channel_id=1, source_target_pairs={{0,2},{1,3},{2,0},{3,1},{4,6},{5,7},{6,4},{7,5},{8,10},{9,11},{10,... | collective-permute-start | bytes 1572872 | tf_op jit(solution)/shard_map/gather_grad_block2/ppermute | solution.py:54
  17.9 16.0 %collective-permute-start.4 = (bf16[64,2048]{1,0:T(8,128)(2,1)S(1)}, bf16[64,2048]{1,0:T(8,128)(2,1)S(1)}, u32[]{:S(2)}, u32[]{:S(2)}) collective-permute-start(bf16[64,2048]{1,0:T(8,128)(2,1)S(1)} %get-tuple-element.44.refs_4_), channel_id=1, source_target_pairs={{0,1},{1,0},{2,3},{3,2},{4,5},{5,4},{6,7},{7,6},{8,9},{9,8},{10,11... | collective-permute-start | bytes 786440 | tf_op jit(solution)/shard_map/gather_saved_block3_row0/ppermute | solution.py:54
  18.3 16.6 %collective-permute-start.5 = (bf16[64,2048]{1,0:T(8,128)(2,1)S(1)}, bf16[64,2048]{1,0:T(8,128)(2,1)S(1)}, u32[]{:S(2)}, u32[]{:S(2)}) collective-permute-start(bf16[64,2048]{1,0:T(8,128)(2,1)S(1)} %get-tuple-element.45.refs_5_), channel_id=1, source_target_pairs={{0,2},{1,3},{2,0},{3,1},{4,6},{5,7},{6,4},{7,5},{8,10},{9,11},{10,... | collective-permute-start | bytes 786440 | tf_op jit(solution)/shard_map/gather_saved_block3_row64/ppermute | solution.py:54
  29.1 10.0 %collective-permute-start.10 = (bf16[64,2048]{1,0:T(8,128)(2,1)S(1)}, bf16[64,2048]{1,0:T(8,128)(2,1)S(1)}, u32[]{:S(2)}, u32[]{:S(2)}) collective-permute-start(bf16[64,2048]{1,0:T(8,128)(2,1)S(1)} %get-tuple-element.51), channel_id=1, source_target_pairs={{0,1},{1,0},{2,3},{3,2},{4,5},{5,4},{6,7},{7,6},{8,9},{9,8},{10,11... | collective-permute-start | bytes 786440 | tf_op jit(solution)/shard_map/gather_grad_block3_row0/ppermute | solution.py:54
  29.6 11.0 %collective-permute-start.11 = (bf16[64,2048]{1,0:T(8,128)(2,1)S(1)}, bf16[64,2048]{1,0:T(8,128)(2,1)S(1)}, u32[]{:S(2)}, u32[]{:S(2)}) collective-permute-start(bf16[64,2048]{1,0:T(8,128)(2,1)S(1)} %get-tuple-element.52), channel_id=1, source_target_pairs={{0,2},{1,3},{2,0},{3,1},{4,6},{5,7},{6,4},{7,5},{8,10},{9,11},{10,... | collective-permute-start | bytes 786440 | tf_op jit(solution)/shard_map/gather_grad_block3_row64/ppermute | solution.py:54
  30.8 15.4 %collective-permute-start.8 = (bf16[64,2048]{1,0:T(8,128)(2,1)S(1)}, bf16[64,2048]{1,0:T(8,128)(2,1)S(1)}, u32[]{:S(2)}, u32[]{:S(2)}) collective-permute-start(bf16[64,2048]{1,0:T(8,128)(2,1)S(1)} %get-tuple-element.46.refs_0_), channel_id=1, source_target_pairs={{0,2},{1,3},{2,0},{3,1},{4,6},{5,7},{6,4},{7,5},{8,10},{9,11},{10,... | collective-permute-start | bytes 786440 | tf_op jit(solution)/shard_map/gather_input_block2_first0/ppermute | solution.py:54
  33.8 12.4 %collective-permute-start.7 = (bf16[64,2048]{1,0:T(8,128)(2,1)S(1)}, bf16[64,2048]{1,0:T(8,128)(2,1)S(1)}, u32[]{:S(2)}, u32[]{:S(2)}) collective-permute-start(bf16[64,2048]{1,0:T(8,128)(2,1)S(1)} %get-tuple-element.47.refs_1_), channel_id=1, source_target_pairs={{0,1},{1,0},{2,3},{3,2},{4,5},{5,4},{6,7},{7,6},{8,9},{9,8},{10,11... | collective-permute-start | bytes 786440 | tf_op jit(solution)/shard_map/gather_input_block1_first64/ppermute | solution.py:54
  35.0 5.6 %copy-start.8 = (bf16[1,2048,512]{2,1,0:T(8,128)(2,1)S(1)}, bf16[1,2048,512]{2,1,0:T(8,128)(2,1)}, u32[]{:S(2)}) copy-start(bf16[1,2048,512]{2,1,0:T(8,128)(2,1)} %param.15) | copy-start | bytes 6291460
  38.7 13.6 %collective-permute-start.6 = (bf16[64,2048]{1,0:T(8,128)(2,1)S(1)}, bf16[64,2048]{1,0:T(8,128)(2,1)S(1)}, u32[]{:S(2)}, u32[]{:S(2)}) collective-permute-start(bf16[64,2048]{1,0:T(8,128)(2,1)S(1)} %get-tuple-element.49), channel_id=1, source_target_pairs={{0,1},{1,0},{2,3},{3,2},{4,5},{5,4},{6,7},{7,6},{8,9},{9,8},{10,11... | collective-permute-start | bytes 786440 | tf_op jit(solution)/shard_map/gather_input_block1_first0/ppermute | solution.py:54
  39.1 13.6 %collective-permute-start.9 = (bf16[64,2048]{1,0:T(8,128)(2,1)S(1)}, bf16[64,2048]{1,0:T(8,128)(2,1)S(1)}, u32[]{:S(2)}, u32[]{:S(2)}) collective-permute-start(bf16[64,2048]{1,0:T(8,128)(2,1)S(1)} %get-tuple-element.50), channel_id=1, source_target_pairs={{0,2},{1,3},{2,0},{3,1},{4,6},{5,7},{6,4},{7,5},{8,10},{9,11},{10,... | collective-permute-start | bytes 786440 | tf_op jit(solution)/shard_map/gather_input_block2_first64/ppermute | solution.py:54
  46.3 9.6 %collective-permute-start.12 = (bf16[64,2048]{1,0:T(8,128)(2,1)S(1)}, bf16[64,2048]{1,0:T(8,128)(2,1)S(1)}, u32[]{:S(2)}, u32[]{:S(2)}) collective-permute-start(bf16[64,2048]{1,0:T(8,128)(2,1)S(1)} %get-tuple-element.56.refs_6_), channel_id=1, source_target_pairs={{0,1},{1,0},{2,3},{3,2},{4,5},{5,4},{6,7},{7,6},{8,9},{9,8},{10,11... | collective-permute-start | bytes 786440 | tf_op jit(solution)/shard_map/gather_input_block3_row0/ppermute | solution.py:54
  47.5 9.6 %collective-permute-start.13 = (bf16[64,2048]{1,0:T(8,128)(2,1)S(1)}, bf16[64,2048]{1,0:T(8,128)(2,1)S(1)}, u32[]{:S(2)}, u32[]{:S(2)}) collective-permute-start(bf16[64,2048]{1,0:T(8,128)(2,1)S(1)} %get-tuple-element.57.refs_7_), channel_id=1, source_target_pairs={{0,2},{1,3},{2,0},{3,1},{4,6},{5,7},{6,4},{7,5},{8,10},{9,11},{10,... | collective-permute-start | bytes 786440 | tf_op jit(solution)/shard_map/gather_input_block3_row64/ppermute | solution.py:54
  51.2 18.6 %collective-permute-start.17 = (bf16[128,2048]{1,0:T(8,128)(2,1)S(1)}, bf16[128,2048]{1,0:T(8,128)(2,1)S(1)}, u32[]{:S(2)}, u32[]{:S(2)}) collective-permute-start(bf16[128,2048]{1,0:T(8,128)(2,1)S(1)} %get-tuple-element.70), channel_id=1, source_target_pairs={{0,1},{1,0},{2,3},{3,2},{4,5},{5,4},{6,7},{7,6},{8,9},{9,8},{10,11... | collective-permute-start | bytes 1572872 | tf_op jit(solution)/shard_map/scatter_grad_block3_part0/ppermute | solution.py:54
  52.2 17.6 %collective-permute-start.18 = (bf16[128,2048]{1,0:T(8,128)(2,1)S(1)}, bf16[128,2048]{1,0:T(8,128)(2,1)S(1)}, u32[]{:S(2)}, u32[]{:S(2)}) collective-permute-start(bf16[128,2048]{1,0:T(8,128)(2,1)S(1)} %get-tuple-element.71), channel_id=1, source_target_pairs={{0,2},{1,3},{2,0},{3,1},{4,6},{5,7},{6,4},{7,5},{8,10},{9,11},{10,... | collective-permute-start | bytes 1572872 | tf_op jit(solution)/shard_map/scatter_grad_block3_part1/ppermute | solution.py:54
  63.8 16.0 %collective-permute-start.14 = (bf16[128,2048]{1,0:T(8,128)(2,1)S(1)}, bf16[128,2048]{1,0:T(8,128)(2,1)S(1)}, u32[]{:S(2)}, u32[]{:S(2)}) collective-permute-start(bf16[128,2048]{1,0:T(8,128)(2,1)S(1)} %get-tuple-element.61), channel_id=1, source_target_pairs={{0,4},{1,5},{2,6},{3,7},{4,8},{5,9},{6,10},{7,11},{8,12},{9,13},{1... | collective-permute-start | bytes 1572872 | tf_op jit(solution)/shard_map/ppermute | solution.py:64
  68.3 8.3 %collective-permute-start.16 = (bf16[64,2048]{1,0:T(8,128)(2,1)S(1)}, bf16[64,2048]{1,0:T(8,128)(2,1)S(1)}, u32[]{:S(2)}, u32[]{:S(2)}) collective-permute-start(bf16[64,2048]{1,0:T(8,128)(2,1)S(1)} %get-tuple-element.65), channel_id=1, source_target_pairs={{0,2},{1,3},{2,0},{3,1},{4,6},{5,7},{6,4},{7,5},{8,10},{9,11},{10,... | collective-permute-start | bytes 786440 | tf_op jit(solution)/shard_map/scatter_branch_block3_part1/ppermute | solution.py:54
  69.6 8.2 %collective-permute-start.15 = (bf16[64,2048]{1,0:T(8,128)(2,1)S(1)}, bf16[64,2048]{1,0:T(8,128)(2,1)S(1)}, u32[]{:S(2)}, u32[]{:S(2)}) collective-permute-start(bf16[64,2048]{1,0:T(8,128)(2,1)S(1)} %get-tuple-element.64.refs_4_), channel_id=1, source_target_pairs={{0,1},{1,0},{2,3},{3,2},{4,5},{5,4},{6,7},{7,6},{8,9},{9,8},{10,11... | collective-permute-start | bytes 786440 | tf_op jit(solution)/shard_map/scatter_branch_block3_part0/ppermute | solution.py:54
  69.9 13.5 %copy-start.6 = (f32[1,128,2048]{2,1,0:T(8,128)S(1)}, f32[1,128,2048]{2,1,0:T(8,128)}, u32[]{:S(2)}) copy-start(f32[1,128,2048]{2,1,0:T(8,128)} %param.9) | copy-start | bytes 3145732
  69.9 13.5 %copy-start.9 = (f32[128,1]{1,0:T(8,128)S(1)}, f32[128,1]{1,0:T(8,128)}, u32[]{:S(2)}) copy-start(f32[128,1]{1,0:T(8,128)} %get-tuple-element.78.inv_ref) | copy-start | bytes 1540
  69.9 12.0 %collective-permute-start.22 = (bf16[64,2048]{1,0:T(8,128)(2,1)S(1)}, bf16[64,2048]{1,0:T(8,128)(2,1)S(1)}, u32[]{:S(2)}, u32[]{:S(2)}) collective-permute-start(bf16[64,2048]{1,0:T(8,128)(2,1)S(1)} %get-tuple-element.72.refs_4_), channel_id=1, source_target_pairs={{0,2},{1,3},{2,0},{3,1},{4,6},{5,7},{6,4},{7,5},{8,10},{9,11},{10,... | collective-permute-start | bytes 786440 | tf_op jit(solution)/shard_map/scatter_grad_block2_part0/ppermute | solution.py:54
  70.2 13.2 %collective-permute-start.21 = (bf16[64,2048]{1,0:T(8,128)(2,1)S(1)}, bf16[64,2048]{1,0:T(8,128)(2,1)S(1)}, u32[]{:S(2)}, u32[]{:S(2)}) collective-permute-start(bf16[64,2048]{1,0:T(8,128)(2,1)S(1)} %get-tuple-element.73.refs_5_), channel_id=1, source_target_pairs={{0,1},{1,0},{2,3},{3,2},{4,5},{5,4},{6,7},{7,6},{8,9},{9,8},{10,11... | collective-permute-start | bytes 786440 | tf_op jit(solution)/shard_map/scatter_grad_block1_part1/ppermute | solution.py:54
  77.9 14.9 %collective-permute-start.19 = (bf16[128,2048]{1,0:T(8,128)(2,1)S(1)}, bf16[128,2048]{1,0:T(8,128)(2,1)S(1)}, u32[]{:S(2)}, u32[]{:S(2)}) collective-permute-start(bf16[128,2048]{1,0:T(8,128)(2,1)S(1)} %get-tuple-element.74.refs_5_), channel_id=1, source_target_pairs={{0,6},{1,7},{2,4},{3,5},{4,10},{5,11},{6,8},{7,9},{8,14},{9,15},{1... | collective-permute-start | bytes 1572872 | tf_op jit(solution)/shard_map/scatter_branch_block2_part0/ppermute | solution.py:64
  79.0 16.4 %collective-permute-start.20 = (bf16[128,2048]{1,0:T(8,128)(2,1)S(1)}, bf16[128,2048]{1,0:T(8,128)(2,1)S(1)}, u32[]{:S(2)}, u32[]{:S(2)}) collective-permute-start(bf16[128,2048]{1,0:T(8,128)(2,1)S(1)} %get-tuple-element.75.refs_6_), channel_id=1, source_target_pairs={{0,5},{1,4},{2,7},{3,6},{4,9},{5,8},{6,11},{7,10},{8,13},{9,12},{1... | collective-permute-start | bytes 1572872 | tf_op jit(solution)/shard_map/scatter_branch_block1_part0/ppermute | solution.py:64
  84.0 14.8 %collective-permute-start.23 = (bf16[128,2048]{1,0:T(8,128)(2,1)S(1)}, bf16[128,2048]{1,0:T(8,128)(2,1)S(1)}, u32[]{:S(2)}, u32[]{:S(2)}) collective-permute-start(bf16[128,2048]{1,0:T(8,128)(2,1)S(1)} %input_grad.1), channel_id=1, source_target_pairs={{0,28},{4,0},{8,4},{12,8},{16,12},{20,16},{24,20},{28,24},{1,29},{... | collective-permute-start | bytes 1572872 | tf_op jit(solution)/shard_map/ppermute | solution.py:70
